TPU v7x, 128 devices: a whole 4x4x4 slice. The times are simulated.
128 devices in a mesh: row: 8 (over z, x_lo), col: 16 (over y, x_hi, core).
Axes of the slice: x: 4 (x_hi: 2, x_lo: 2; x = x_hi * 2 + x_lo), y: 4, z: 4, core: 2. Of those that a mesh axis runs over, the one named last changes fastest.
Arguments:
- kernel: float32 [16384, 16384], P(('row', 'col')), may hold values from -1 to 6, as said below
- start_block: float32 [16384, 128], P(('row', 'col')), may hold values from -6 to 6
- test_kernel: float32 [16384, 256], P(('row', 'col')), may hold values from -67.88225 to 67.88225
- cutoff: int32 [1], replicated, may hold values from 32 to 128
Outputs:
- subspace: float32 [16384, 128], P(('row', 'col'))
- projection: float32 [16384, 256], P(('row', 'col'))
Inputs may be any that keep to these rules, and one draw needn't show every extreme that they name: `kernel`: symmetric.
All inputs are finite; a program needn't handle non-finite values.
Results may differ from a plain program's by a relative error of at most 0.0003.
Values sent between devices are 32-bit elements; how exact they have to be, the bound alone decides.
A program may use at most 128 MiB of HBM per device.

v0:
```python
import jax
import jax.numpy as jnp
from jax import lax
from jax.sharding import PartitionSpec as P

BLOCK_WIDTH = 128
ITERATIONS = 4


def orthonormal(image):
    local_gram = jnp.dot(
        image.T, image, precision=lax.Precision.HIGHEST, preferred_element_type=jnp.float32
    )
    gram = lax.psum(local_gram, ("row", "col"))
    lower = jnp.linalg.cholesky(gram)
    identity = jnp.eye(gram.shape[0], dtype=jnp.float32)
    inverse = lax.linalg.triangular_solve(lower, identity, left_side=True, lower=True)
    return jnp.dot(
        image, inverse.T, precision=lax.Precision.HIGHEST, preferred_element_type=jnp.float32
    )


def per_device(kernel, start_block, test_kernel, cutoff):
    block = start_block
    for step in range(ITERATIONS):
        image = jnp.dot(
            kernel,
            lax.all_gather(block, ("row", "col"), axis=0, tiled=True),
            precision=lax.Precision.HIGHEST,
            preferred_element_type=jnp.float32,
        )
        block = orthonormal(image)
    local_coefficients = jnp.dot(
        block.T, test_kernel, precision=lax.Precision.HIGHEST, preferred_element_type=jnp.float32
    )
    coefficients = lax.psum(local_coefficients, ("row", "col"))
    keep = (jnp.arange(BLOCK_WIDTH) < cutoff[0]).astype(jnp.float32)
    coefficients = coefficients * keep[:, None]
    projection = jnp.dot(
        block, coefficients, precision=lax.Precision.HIGHEST, preferred_element_type=jnp.float32
    )
    return (block, projection)


def solution(mesh):
    in_specs = (P(("row", "col"), None), P(("row", "col"), None), P(("row", "col"), None), P())
    out_specs = (P(("row", "col"), None), P(("row", "col"), None))
    return jax.shard_map(
        per_device, mesh=mesh, in_specs=in_specs, out_specs=out_specs, check_vma=False
    )
```

profile of v0, /device:TPU:1, one launch (start us, length us, event | category | flops | bytes accessed | tf_op | source)
XLA Modules:
  0.0 1679.2 jit_solution(13577950380398083879)
XLA Ops:
  8.0 207.9 %all-gather.5.cloned.1.call-done = f32[16384,128]{1,0:T(8,128)} async-done(((f32[128,128]{1,0:T(8,128)}), f32[16384,128]{1,0:T(8,128)}) %all-gather.5.cloned.1.call-update) | async-done | bytes 8388624 | tf_op jit(solution)/shard_map/all_gather | solution.py:28
  215.8 11.8 fusion.23
  227.6 0.9 fusion.24
  228.6 136.7 %all-reduce.6.cloned.1.call-done = f32[128,128]{0,1:T(8,128)} async-done(((f32[128,128]{0,1:T(8,128)}), f32[128,128]{0,1:T(8,128)}) %all-reduce.6.cloned.1.call-update) | async-done | bytes 65552 | tf_op jit(solution)/shard_map/psum | solution.py:14
  365.3 0.9 copy.7
  367.1 11.7 cholesky.74
  380.2 9.8 custom-call.8
  390.3 0.9 fusion.25
  391.4 199.9 %all-gather.7.cloned.1.call-done = f32[16384,128]{1,0:T(8,128)} async-done(((f32[128,128]{1,0:T(8,128)}), f32[16384,128]{1,0:T(8,128)}) %all-gather.7.cloned.1.call-update) | async-done | bytes 8388624 | tf_op jit(solution)/shard_map/all_gather | solution.py:28
  591.4 17.0 %fusion.26 = f32[128,128]{1,0:T(8,128)S(1)} fusion(f32[16384,128]{1,0:T(8,128)} %all-gather.7.cloned.1.call-done, f32[128,16384]{1,0:T(8,128)} %param.7), kind=kOutput, calls=%fused_computation.45 | convolution fusion | flops 3221225472 | bytes 16842752 | tf_op jit(solution)/shard_map/dot_general | solution.py:26
  608.3 0.9 fusion.27
  609.5 136.5 %all-reduce.8.cloned.1.call-done = f32[128,128]{0,1:T(8,128)} async-done(((f32[128,128]{0,1:T(8,128)}), f32[128,128]{0,1:T(8,128)}) %all-reduce.8.cloned.1.call-update) | async-done | bytes 65552 | tf_op jit(solution)/shard_map/psum | solution.py:14
  746.0 0.9 copy.9
  747.8 11.7 cholesky.85
  760.8 9.8 custom-call.9
  770.9 0.9 fusion.28
  772.2 199.9 %all-gather.9.cloned.1.call-done = f32[16384,128]{1,0:T(8,128)} async-done(((f32[128,128]{1,0:T(8,128)}), f32[16384,128]{1,0:T(8,128)}) %all-gather.9.cloned.1.call-update) | async-done | bytes 8388624 | tf_op jit(solution)/shard_map/all_gather | solution.py:28
  972.0 17.0 %fusion.29 = f32[128,128]{1,0:T(8,128)S(1)} fusion(f32[16384,128]{1,0:T(8,128)} %all-gather.9.cloned.1.call-done, f32[128,16384]{1,0:T(8,128)} %param.7), kind=kOutput, calls=%fused_computation.48 | convolution fusion | flops 3221225472 | bytes 16842752 | tf_op jit(solution)/shard_map/dot_general | solution.py:26
  990.3 136.3 %all-reduce.10.cloned.1.call-done = f32[128,128]{0,1:T(8,128)} async-done(((f32[128,128]{0,1:T(8,128)}), f32[128,128]{0,1:T(8,128)}) %all-reduce.10.cloned.1.call-update) | async-done | bytes 65552 | tf_op jit(solution)/shard_map/psum | solution.py:14
  1126.6 0.9 copy.11
  1128.4 11.7 cholesky.96
  1141.4 9.8 custom-call.10
  1151.6 0.9 fusion.31
  1153.1 199.6 %all-gather.11.cloned.1.call-done = f32[16384,128]{1,0:T(8,128)} async-done(((f32[128,128]{1,0:T(8,128)}), f32[16384,128]{1,0:T(8,128)}) %all-gather.11.cloned.1.call-update) | async-done | bytes 8388624 | tf_op jit(solution)/shard_map/all_gather | solution.py:28
  1352.6 17.0 %fusion.32 = f32[128,128]{1,0:T(8,128)S(1)} fusion(f32[16384,128]{1,0:T(8,128)} %all-gather.11.cloned.1.call-done, f32[128,16384]{1,0:T(8,128)} %param.7), kind=kOutput, calls=%fused_computation.51 | convolution fusion | flops 3221225472 | bytes 16842752 | tf_op jit(solution)/shard_map/dot_general | solution.py:26
  1371.4 135.8 %all-reduce.12.cloned.1.call-done = f32[128,128]{0,1:T(8,128)} async-done(((f32[128,128]{0,1:T(8,128)}), f32[128,128]{0,1:T(8,128)}) %all-reduce.12.cloned.1.call-update) | async-done | bytes 65552 | tf_op jit(solution)/shard_map/psum | solution.py:14
  1507.2 0.9 copy.13
  1509.0 11.7 cholesky.107
  1522.0 9.8 custom-call.11
  1532.5 1.0 fusion.35
  1533.5 137.1 %all-reduce.14.cloned.1.call-done = f32[128,256]{1,0:T(8,128)} async-done(((f32[128,256]{1,0:T(8,128)}), f32[128,256]{1,0:T(8,128)}) %all-reduce.14.cloned.1.call-update) | async-done | bytes 131088 | tf_op jit(solution)/shard_map/psum | solution.py:36
  1670.5 1.9 fusion.8
  (46 shorter events, 14.8 us)
Async XLA Ops:
  7.2 1525.3 %copy-start = (f32[128,256]{1,0:T(8,128)S(1)}, f32[128,256]{1,0:T(8,128)}, u32[]{:S(2)}) copy-start(f32[128,256]{1,0:T(8,128)} %param.9) | copy-start | bytes 393220
  7.2 208.6 %all-gather.5.cloned.1.call-start = ((), (), s32[]{:S(2)}) async-start(), calls=%async_computation | async-start | bytes 8454144 | tf_op jit(solution)/shard_map/all_gather | solution.py:28
  7.9 357.4 %all-reduce.6.cloned.1.call-start = ((), (), s32[]{:S(2)}) async-start(), calls=%async_computation.1 | async-start | bytes 131072 | tf_op jit(solution)/shard_map/psum | solution.py:14
  228.6 362.8 %all-gather.7.cloned.1.call-start = ((), (), s32[]{:S(2)}) async-start(), calls=%async_computation.2 | async-start | bytes 8454144 | tf_op jit(solution)/shard_map/all_gather | solution.py:28
  391.2 354.8 %all-reduce.8.cloned.1.call-start = ((), (), s32[]{:S(2)}) async-start(), calls=%async_computation.3 | async-start | bytes 131072 | tf_op jit(solution)/shard_map/psum | solution.py:14
  609.3 362.8 %all-gather.9.cloned.1.call-start = ((), (), s32[]{:S(2)}) async-start(), calls=%async_computation.4 | async-start | bytes 8454144 | tf_op jit(solution)/shard_map/all_gather | solution.py:28
  771.9 354.7 %all-reduce.10.cloned.1.call-start = ((), (), s32[]{:S(2)}) async-start(), calls=%async_computation.5 | async-start | bytes 131072 | tf_op jit(solution)/shard_map/psum | solution.py:14
  989.9 362.7 %all-gather.11.cloned.1.call-start = ((), (), s32[]{:S(2)}) async-start(), calls=%async_computation.6 | async-start | bytes 8454144 | tf_op jit(solution)/shard_map/all_gather | solution.py:28
  1152.5 354.7 %all-reduce.12.cloned.1.call-start = ((), (), s32[]{:S(2)}) async-start(), calls=%async_computation.7 | async-start | bytes 131072 | tf_op jit(solution)/shard_map/psum | solution.py:14
  1370.5 300.0 %all-reduce.14.cloned.1.call-start = ((), (), s32[]{:S(2)}) async-start(), calls=%async_computation.8 | async-start | bytes 262144 | tf_op jit(solution)/shard_map/psum | solution.py:36
  1532.5 140.0 %copy-start.1 = (f32[128,128]{1,0:T(8,128)}, f32[128,128]{1,0:T(8,128)S(1)}, u32[]{:S(2)}) copy-start(f32[128,128]{1,0:T(8,128)S(1)} %fusion.34) | copy-start | bytes 196612
Sparse Core Ops, SparseCore 0:
  9.7 206.0 all-gather.4
  228.7 136.5 all-reduce.5
  391.3 199.9 all-gather.6
  609.4 136.5 all-reduce.7
  772.0 199.9 all-gather.8
  990.1 136.4 all-reduce.9
  1152.6 199.9 all-gather.10
  1370.7 136.4 all-reduce.11
  1533.6 136.9 all-reduce.13
where the time goes:
time: 1690 us; the launch traced here: 1680 us
  waiting for transfers between devices  1490 us (88%)
  other arithmetic  94.8 us (6%)
  matrix products  73.3 us (4%)
    all_gather x4, waiting for transfers between devices, per_device(): lax.all_gather(block, ('row', 'col'), axis=0, tiled=True)  807 us
    psum x4, waiting for transfers between devices, orthonormal(): gram = lax.psum(local_gram, ('row', 'col'))  545 us
    psum x1, waiting for transfers between devices, per_device(): coefficients = lax.psum(local_coefficients, ('row', 'col'))  137 us
    dot_general x4, matrix products, per_device(): jnp.dot(kernel, lax.all_gather(block, ('row', 'col'), axis=0, tiled=True)...  62.7 us
    another operation x12, other arithmetic, orthonormal(): lower = jnp.linalg.cholesky(gram)  49.6 us
    another operation x8, other arithmetic, orthonormal(): lax.linalg.triangular_solve(lower, identity, left_side=True, lower=True)  41.9 us
  transfers between devices with their start and end apart: 9, of which 9 were waited for; matrix products, arithmetic and copies ran while one was open for 0% of the time, Pallas kernels for 0%

commit v1 on v0

v1 whole, which is shorter than its diff:
```python
import functools
import itertools

import jax
import jax.numpy as jnp
from jax import lax
from jax.experimental import pallas as pl
from jax.experimental.pallas import tpu as pltpu
from jax.sharding import PartitionSpec as P

BLOCK = 128
TEST = 256
ITERATIONS = 4
RING = 4
SLOTS = RING**3
CHUNK = 8
HALF = BLOCK // 2
MESH = pl.DeviceIdType.MESH
HIGHEST = lax.Precision.HIGHEST
STEPS = [(axis, sign) for axis in range(3) for sign in (1, -1)]


def spanning_tree():
    depth = lambda d: sum(min(c, RING - c) for c in d)

    def options(d):
        found = []
        for label, (axis, sign) in enumerate(STEPS):
            before = list(d)
            before[axis] = (before[axis] - sign) % RING
            if depth(before) == depth(d) - 1:
                found.append((label, tuple(before)))
        return found

    points = sorted(itertools.product(range(RING), repeat=3), key=lambda d: (depth(d), d))
    choice = {d: options(d)[0] for d in points[1:]}

    def cost():
        whole, level, degree = {}, {}, {}
        for d, (label, parent) in choice.items():
            whole[label] = whole.get(label, 0) + 1
            level[depth(d), label] = level.get((depth(d), label), 0) + 1
            degree[parent] = degree.get(parent, 0) + 1
        square = lambda counts: sum(v * v for v in counts.values())
        return 4 * square(whole) + 2 * square(level) + square(degree)

    best, changed = cost(), True
    while changed:
        changed = False
        for d in points[1:]:
            for option in options(d):
                kept = choice[d]
                choice[d] = option
                now = cost()
                if now < best:
                    best, changed = now, True
                else:
                    choice[d] = kept
    order = points[:1]
    for level in range(1, 7):
        rest = [d for d in points if depth(d) == level]
        seen = {}
        ranked = []
        for d in rest:
            label = choice[d][0]
            seen[label] = seen.get(label, 0) + 1
            ranked.append((order.index(choice[d][1]), seen[label], label, d))
        order += [d for *_, d in sorted(ranked)]
    slot = {d: i for i, d in enumerate(order)}
    children = [[] for _ in order]
    for d in order[1:]:
        label, parent = choice[d]
        children[slot[parent]].append((slot[d], label))
    return order, children


ORDER, CHILDREN = spanning_tree()


def exact_dot(a, b, dims=(((1,), (0,)), ((), ()))):
    return lax.dot_general(a, b, dims, precision=HIGHEST, preferred_element_type=jnp.float32)


def eliminate(m, inverse, panel):
    base = 8 * panel
    wide = (8, BLOCK)
    lane = lax.broadcasted_iota(jnp.int32, wide, 1)
    within = (lane >= base) & (lane < base + 8)
    top = m[base : base + 8, :]
    raw = [jnp.broadcast_to(top[k : k + 1, :], wide) for k in range(8)]
    a = {
        (k, i): jnp.broadcast_to(raw[k][:, base + i : base + i + 1], wide) for k in range(8) for i in range(k, 8)
    }
    rows = [jnp.where(within, jnp.where(lane == base + k, 1.0, 0.0), raw[k]) for k in range(8)]
    over, factor = [], {}
    for k in range(8):
        over.append(1.0 / a[k, k])
        for i in range(k + 1, 8):
            factor[k, i] = a[k, i] * over[k]
            for j in range(i, 8):
                a[i, j] = a[i, j] - factor[k, i] * a[k, j]
            rows[i] = rows[i] - factor[k, i] * rows[k]
    for k in range(8):
        done = jnp.where(lane < base + 8, rows[k] * (over[k] * jnp.sqrt(a[k, k])), 0.0)
        inverse[base + k : base + k + 1, :] = done[0:1, :]
    if panel == BLOCK // 8 - 1:
        return
    solved = [rows[k] * over[k] for k in range(8)]
    for k in reversed(range(8)):
        for i in range(k):
            solved[i] = solved[i] - factor[i, k] * solved[k]
    for r in range(base + 8, BLOCK, 8):
        rest = m[r : r + 8, :]
        terms = [jnp.broadcast_to(rest[:, base + k : base + k + 1], wide) * solved[k] for k in range(8)]
        while len(terms) > 1:
            terms = [x + y for x, y in zip(terms[::2], terms[1::2])]
        m[r : r + 8, :] = jnp.where(within, 0.0, rest) - terms[0]


def kernel(
    kernel_hbm, start, test, cutoff, subspace, projection,
    buf, kf, khl, acc, m, inverse, loc, sib, lines, full, cloc, csib, clines, cfull, psend, precv,
    ag_recv, ag_send, k_local, k_recv, k_send, ar_recv, ar_send, cr_recv, cr_send, p_recv, p_send,
):
    row, col = lax.axis_index("row"), lax.axis_index("col")
    core = lax.rem(col, 2)
    here = (
        lax.rem(lax.div(col, 2), 2) * 2 + lax.rem(row, 2),
        lax.div(col, 4),
        lax.div(row, 2),
    )

    def device(x, y, z, c):
        return (z * 2 + lax.rem(x, 2), (y * 2 + lax.div(x, 2)) * 2 + c)

    def moved(axis, by):
        place = list(here)
        place[axis] = lax.rem(place[axis] + by, RING)
        return device(*place, core)

    sibling = device(*here, 1 - core)
    neighbours = [moved(axis, 1 if sign > 0 else RING - 1) for axis, sign in STEPS]

    barrier = pltpu.get_barrier_semaphore()
    greet = [moved(axis, by) for axis in range(3) for by in (1, 2, 3)] + [sibling]
    for other in greet:
        pl.semaphore_signal(barrier, inc=1, device_id=other, device_id_type=MESH)
    pl.semaphore_wait(barrier, len(greet))

    def remote(src, dst, send, recv, to):
        return pltpu.make_async_remote_copy(
            src_ref=src, dst_ref=dst, send_sem=send, recv_sem=recv, device_id=to, device_id_type=MESH
        )

    def block(par, s):
        return buf.at[par, pl.ds(s * BLOCK, BLOCK)]

    def forward(par, s):
        for child, label in CHILDREN[s]:
            remote(
                block(par, s), block(par, child), ag_send, ag_recv.at[par, child], neighbours[label]
            ).start()

    def arrived(par, s):
        pltpu.make_async_copy(block(par, s), block(par, s), ag_recv.at[par, s]).wait()

    def columns(s, c):
        x, y, z = [lax.rem(p + RING - d, RING) for p, d in zip(here, ORDER[s])]
        r, q = device(x, y, z, c)
        return pl.ds(pl.multiple_of((r * 16 + q) * BLOCK, BLOCK), BLOCK)

    def lanes(c):
        return pl.ds(c * CHUNK * BLOCK, CHUNK * BLOCK)

    def start_kernel_copies(s):
        c, there = s // CHUNK, pl.ds(s * BLOCK, BLOCK)
        remote(
            kernel_hbm.at[:, columns(s, 1 - core)], kf.at[pl.ds(BLOCK, BLOCK), there],
            k_send.at[c], k_recv.at[c], sibling,
        ).start()
        pltpu.make_async_copy(
            kernel_hbm.at[:, columns(s, core)], kf.at[pl.ds(0, BLOCK), there], k_local.at[c]
        ).start()

    def split_kernel(c):
        own, other = kf.at[pl.ds(0, BLOCK), lanes(c)], kf.at[pl.ds(BLOCK, BLOCK), lanes(c)]
        pltpu.make_async_copy(own, own, k_local.at[c]).wait()
        pltpu.make_async_copy(other, other, k_recv.at[c]).wait()
        value = kf[:, lanes(c)]
        high = value.astype(jnp.bfloat16)
        khl[0 : 2 * BLOCK, lanes(c)] = high
        khl[2 * BLOCK : 4 * BLOCK, lanes(c)] = (value - high.astype(jnp.float32)).astype(jnp.bfloat16)

    def multiply(par, c):
        x = buf[par, pl.ds(c * CHUNK * BLOCK, CHUNK * BLOCK), :]
        high = x.astype(jnp.bfloat16)
        low = (x - high.astype(jnp.float32)).astype(jnp.bfloat16)
        term = jnp.dot(
            khl[:, lanes(c)], jnp.concatenate([high, low], axis=1), preferred_element_type=jnp.float32
        )
        if c == 0:
            acc[...] = term
        else:
            acc[...] += term

    def sum_stages(loc, sib, lines, full, recv, send):
        kept = pl.ds(pl.multiple_of(core * HALF, HALF), HALF)
        given = pl.ds(pl.multiple_of((1 - core) * HALF, HALF), HALF)
        sent = []

        def start(src, dst, index, to):
            copy = remote(src, dst, send.at[index], recv.at[index], to)
            copy.start()
            sent.append(copy)

        def wait(ref, index):
            pltpu.make_async_copy(ref, ref, recv.at[index]).wait()

        def to_line(axis, value):
            mine = lines.at[axis, here[axis]]
            mine[...] = value
            for by in (1, 2, 3):
                start(mine, mine, 1 + 3 * axis + by - 1, moved(axis, by))

        def from_line(axis):
            for by in (1, 2, 3):
                wait(lines.at[axis, lax.rem(here[axis] + RING - by, RING)], 1 + 3 * axis + by - 1)
            return (lines[axis, 0] + lines[axis, 1]) + (lines[axis, 2] + lines[axis, 3])

        def first():
            start(loc.at[given], sib, 0, sibling)

        def second():
            wait(sib, 0)
            to_line(0, loc[kept, :] + sib[...])

        def fifth():
            full[kept, :] = from_line(2)
            start(full.at[kept], full.at[kept], 10, sibling)

        def last():
            wait(full.at[given], 10)
            for copy in sent:
                copy.wait_send()

        return [
            first, second, lambda: to_line(1, from_line(0)), lambda: to_line(2, from_line(1)), fifth, last
        ]

    def factor_panel(p):
        if p == 0:
            m[...] = full_now[0][...]
        eliminate(m, inverse, p)

    full_now = [None]

    def gather_and_multiply(par, tasks):
        forward(par, 0)
        for s in range(SLOTS):
            if s:
                arrived(par, s)
                forward(par, s)
            for task in tasks.get(s, ()):
                task()
        value = acc[...]
        value = value[:, :BLOCK] + value[:, BLOCK:]
        value = value[: 2 * BLOCK] + value[2 * BLOCK :]
        psend[...] = value[BLOCK:]
        copy = remote(psend, precv.at[par], p_send, p_recv.at[par], sibling)
        copy.start()
        whole = buf.at[par, pl.ds(BLOCK, (SLOTS - 1) * BLOCK)]
        pltpu.make_async_copy(whole, whole, ag_send).wait()
        copy.wait()
        return value[:BLOCK] + precv[par]

    def local_gram(par):
        y = buf[par, pl.ds(0, BLOCK), :]
        loc[...] = exact_dot(y.T, y)

    buf[0, pl.ds(0, BLOCK), :] = start[...]
    tasks = {}
    for s in range(SLOTS):
        tasks.setdefault((s * 2) // 5, []).append(lambda s=s: start_kernel_copies(s))
    for c in range(SLOTS // CHUNK):
        tasks.setdefault(35 + 4 * c, []).extend([lambda c=c: split_kernel(c), lambda c=c: multiply(0, c)])
    image = gather_and_multiply(0, tasks)
    buf[1, pl.ds(0, BLOCK), :] = image
    for c in range(SLOTS // CHUNK):
        given = kf.at[pl.ds(0, BLOCK), lanes(c)]
        pltpu.make_async_copy(given, given, k_send.at[c]).wait()

    def step(t, carry):
        par = lax.rem(t, 2)
        stages = sum_stages(loc, sib.at[par], lines.at[par], full.at[par], ar_recv.at[par], ar_send)
        full_now[0] = full.at[par]
        tasks = {0: [lambda: local_gram(par), stages[0]]}
        for at, stage in zip((0, 12, 26, 38, 44), stages[1:]):
            tasks.setdefault(at, []).append(stage)
        for p in range(16):
            tasks.setdefault(45 + p, []).append(lambda p=p: factor_panel(p))
        for c in range(SLOTS // CHUNK):
            tasks.setdefault((c + 1) * CHUNK - 1, []).append(lambda c=c: multiply(par, c))
        image = gather_and_multiply(par, tasks)
        buf[1 - par, pl.ds(0, BLOCK), :] = exact_dot(image, inverse[...], (((1,), (1,)), ((), ())))
        return carry

    lax.fori_loop(1, ITERATIONS, step, 0)

    par = ITERATIONS % 2
    stages = sum_stages(loc, sib.at[par], lines.at[par], full.at[par], ar_recv.at[par], ar_send)
    late = sum_stages(cloc, csib, clines, cfull, cr_recv, cr_send)
    full_now[0] = full.at[par]
    local_gram(par)
    stages[0]()
    last = buf[par, pl.ds(0, BLOCK), :]
    cloc[...] = exact_dot(last.T, test[...])
    stages[1]()
    for one, two in zip(late[:4], stages[2:]):
        one()
        two()
    for p in range(16):
        if p == 4:
            late[4]()
        if p == 8:
            late[5]()
        factor_panel(p)
    result = exact_dot(buf[par, pl.ds(0, BLOCK), :], inverse[...], (((1,), (1,)), ((), ())))
    subspace[...] = result
    keep = lax.broadcasted_iota(jnp.int32, (BLOCK, TEST), 0) < cutoff[0]
    coefficients = exact_dot(inverse[...], cfull[...]) * jnp.where(keep, 1.0, 0.0)
    projection[...] = exact_dot(result, coefficients)


def per_device(kernel_rows, start_block, test_kernel, cutoff):
    f32 = jnp.float32
    vmem = pl.BlockSpec(memory_space=pltpu.VMEM)
    dma = pltpu.SemaphoreType.DMA
    chunks = SLOTS // CHUNK
    return pl.pallas_call(
        kernel,
        out_shape=(
            jax.ShapeDtypeStruct((BLOCK, BLOCK), f32),
            jax.ShapeDtypeStruct((BLOCK, TEST), f32),
        ),
        in_specs=[pl.BlockSpec(memory_space=pl.ANY), vmem, vmem, pl.BlockSpec(memory_space=pltpu.SMEM)],
        out_specs=(vmem, vmem),
        scratch_shapes=[
            pltpu.VMEM((2, SLOTS * BLOCK, BLOCK), f32),
            pltpu.VMEM((2 * BLOCK, SLOTS * BLOCK), f32),
            pltpu.VMEM((4 * BLOCK, SLOTS * BLOCK), jnp.bfloat16),
            pltpu.VMEM((4 * BLOCK, 2 * BLOCK), f32),
            pltpu.VMEM((BLOCK, BLOCK), f32),
            pltpu.VMEM((BLOCK, BLOCK), f32),
            pltpu.VMEM((BLOCK, BLOCK), f32),
            pltpu.VMEM((2, HALF, BLOCK), f32),
            pltpu.VMEM((2, 3, RING, HALF, BLOCK), f32),
            pltpu.VMEM((2, BLOCK, BLOCK), f32),
            pltpu.VMEM((BLOCK, TEST), f32),
            pltpu.VMEM((HALF, TEST), f32),
            pltpu.VMEM((3, RING, HALF, TEST), f32),
            pltpu.VMEM((BLOCK, TEST), f32),
            pltpu.VMEM((BLOCK, BLOCK), f32),
            pltpu.VMEM((2, BLOCK, BLOCK), f32),
            dma((2, SLOTS)),
            dma,
            dma((chunks,)),
            dma((chunks,)),
            dma((chunks,)),
            dma((2, 11)),
            dma((11,)),
            dma((11,)),
            dma((11,)),
            dma((2,)),
            dma,
        ],
        compiler_params=pltpu.CompilerParams(
            collective_id=0, has_side_effects=True, vmem_limit_bytes=56 * 1024 * 1024
        ),
        cost_estimate=pl.CostEstimate(
            flops=4 * 2 * 512 * 8192 * 256, bytes_accessed=16 * 2**20, transcendentals=0
        ),
        name="iterate",
    )(kernel_rows, start_block, test_kernel, cutoff)


def solution(mesh):
    in_specs = (P(("row", "col"), None), P(("row", "col"), None), P(("row", "col"), None), P())
    out_specs = (P(("row", "col"), None), P(("row", "col"), None))
    return jax.shard_map(
        per_device, mesh=mesh, in_specs=in_specs, out_specs=out_specs, check_vma=False
    )
```

time: 1690 us -> 163 us (0.10)
  waiting for transfers between devices: 1490 us -> 0 us
  Pallas kernels: 0 us -> 158 us
  other arithmetic: 94.8 us -> 0 us
  matrix products: 73.3 us -> 0 us
    all_gather x4 -> x0, waiting for transfers between devices: 807 us -> none  [per_device(): lax.all_gather(block, ('row', 'col'), axis=0, tiled=True)]
    psum x5 -> x0, waiting for transfers between devices: 682 us -> none  [the longest x4 545 us: orthonormal(): gram = lax.psum(local_gram, ('row', 'col'))]
    pallas_call x0 -> x1, Pallas kernels: none -> 158 us  [per_device(): pl.pallas_call(kernel, out_shape=(jax.ShapeDtypeStruct((BLOCK, BLOCK), f3...]
    another operation x20 -> x0, other arithmetic: 91.4 us -> none  [the longest x12 49.6 us: orthonormal(): lower = jnp.linalg.cholesky(gram)]
    dot_general x14 -> x0, matrix products: 72.2 us -> none  [the longest x4 62.7 us: per_device(): jnp.dot(kernel, lax.all_gather(block, ('row', 'col'), axis=0, tiled=True)...]
  transfers between devices with their start and end apart: 9 -> 0, of which waited for: 9 -> 0; matrix products, arithmetic and copies ran while one was open for 0% -> 0% of each run, Pallas kernels for 0% -> 0%
where the time goes in v1:
time: 163 us; the launch traced here: 162 us
  Pallas kernels  158 us (97%)
  local copies, waits for them, and re-layouts  3.04 us (2%)
    pallas_call x1, Pallas kernels, per_device(): pl.pallas_call(kernel, out_shape=(jax.ShapeDtypeStruct((BLOCK, BLOCK), f3...  158 us

profile of v1, /device:TPU:1, one launch (start us, length us, event | category | flops | bytes accessed | tf_op | source)
XLA Modules:
  0.0 162.4 jit_solution(3923478673886080373)
XLA Ops:
  1.3 158.0 %iterate.1 = (f32[128,128]{1,0:T(8,128)}, f32[128,256]{1,0:T(8,128)}) custom-call(f32[128,16384]{1,0:T(8,128)} %kernel_hbm.1, f32[128,128]{1,0:T(8,128)} %start.1, f32[128,256]{1,0:T(8,128)} %test.1, s32[1]{0:T(128)S(6)} %copy.8.cutoff), custom_call_target="tpu_custom_call" | custom-call | flops 8589934592 | bytes 16777216 | tf_op jit(solution)/shard_map/iterate/pallas_call | solution.py:339
  159.3 1.5 copy.9
  160.8 1.6 copy.10

commit v2 on v1

--- a/solution.py
+++ b/solution.py
@@ -1,5 +1,4 @@
 import functools
-import itertools
 
 import jax
 import jax.numpy as jnp
@@ -20,68 +19,48 @@
 STEPS = [(axis, sign) for axis in range(3) for sign in (1, -1)]
 
 
+TREE = (
+    0, 75, 10, 96, 26, 23, 289, 51, 95, 168, 295, 32, 16, 81, 102, 307,
+    122, 363, 47, 192, 58, 369, 71, 126, 199, 177, 332, 343, 41, 376, 355, 267,
+    138, 208, 247, 184, 119, 314, 379, 304, 320, 191, 108, 88, 339, 216, 146, 215,
+    152, 65, 162, 224, 351, 277, 329, 132, 274, 243, 230, 259, 287, 234, 256, 159,
+)
+
+
 def spanning_tree():
-    depth = lambda d: sum(min(c, RING - c) for c in d)
-
-    def options(d):
-        found = []
-        for label, (axis, sign) in enumerate(STEPS):
-            before = list(d)
-            before[axis] = (before[axis] - sign) % RING
-            if depth(before) == depth(d) - 1:
-                found.append((label, tuple(before)))
-        return found
-
-    points = sorted(itertools.product(range(RING), repeat=3), key=lambda d: (depth(d), d))
-    choice = {d: options(d)[0] for d in points[1:]}
-
-    def cost():
-        whole, level, degree = {}, {}, {}
-        for d, (label, parent) in choice.items():
-            whole[label] = whole.get(label, 0) + 1
-            level[depth(d), label] = level.get((depth(d), label), 0) + 1
-            degree[parent] = degree.get(parent, 0) + 1
-        square = lambda counts: sum(v * v for v in counts.values())
-        return 4 * square(whole) + 2 * square(level) + square(degree)
-
-    best, changed = cost(), True
-    while changed:
-        changed = False
-        for d in points[1:]:
-            for option in options(d):
-                kept = choice[d]
-                choice[d] = option
-                now = cost()
-                if now < best:
-                    best, changed = now, True
-                else:
-                    choice[d] = kept
-    order = points[:1]
-    for level in range(1, 7):
-        rest = [d for d in points if depth(d) == level]
-        seen = {}
-        ranked = []
-        for d in rest:
-            label = choice[d][0]
-            seen[label] = seen.get(label, 0) + 1
-            ranked.append((order.index(choice[d][1]), seen[label], label, d))
-        order += [d for *_, d in sorted(ranked)]
-    slot = {d: i for i, d in enumerate(order)}
+    order = [(code // 96, code // 24 % 4, code // 6 % 4) for code in TREE]
+    slot = {d: s for s, d in enumerate(order)}
     children = [[] for _ in order]
-    for d in order[1:]:
-        label, parent = choice[d]
-        children[slot[parent]].append((slot[d], label))
+    height = [0] * len(order)
+    depth = lambda s: sum(min(c, RING - c) for c in order[s])
+    for s in sorted(range(1, len(order)), key=depth, reverse=True):
+        axis, sign = STEPS[TREE[s] % 6]
+        before = list(order[s])
+        before[axis] = (before[axis] - sign) % RING
+        parent = slot[tuple(before)]
+        children[parent].append((s, TREE[s] % 6))
+        height[parent] = max(height[parent], height[s] + 1)
+    for found in children:
+        found.sort(key=lambda child: -height[child[0]])
     return order, children
 
 
 ORDER, CHILDREN = spanning_tree()
+INNER = sum(1 for found in CHILDREN if found)
+GROUP = [s if s < INNER else max(INNER, s // CHUNK * CHUNK) for s in range(SLOTS)]
 
 
 def exact_dot(a, b, dims=(((1,), (0,)), ((), ()))):
     return lax.dot_general(a, b, dims, precision=HIGHEST, preferred_element_type=jnp.float32)
 
 
-def eliminate(m, inverse, panel):
+def reciprocal(x):
+    r = pl.reciprocal(x, approx=True)
+    r = r * (2.0 - x * r)
+    return r * (2.0 - x * r)
+
+
+def eliminate(m, inverse, scale, panel):
     base = 8 * panel
     wide = (8, BLOCK)
     lane = lax.broadcasted_iota(jnp.int32, wide, 1)
@@ -92,34 +71,52 @@
         (k, i): jnp.broadcast_to(raw[k][:, base + i : base + i + 1], wide) for k in range(8) for i in range(k, 8)
     }
     rows = [jnp.where(within, jnp.where(lane == base + k, 1.0, 0.0), raw[k]) for k in range(8)]
-    over, factor = [], {}
-    for k in range(8):
-        over.append(1.0 / a[k, k])
-        for i in range(k + 1, 8):
-            factor[k, i] = a[k, i] * over[k]
+    over, factor = {}, {}
+    for k in range(0, 8, 2):
+        p, q, r = a[k, k], a[k, k + 1], a[k + 1, k + 1]
+        over[k] = reciprocal(p * r - q * q)
+        for i in range(k + 2, 8):
+            factor[k, i] = (r * a[k, i] - q * a[k + 1, i]) * over[k]
+            factor[k + 1, i] = (p * a[k + 1, i] - q * a[k, i]) * over[k]
             for j in range(i, 8):
-                a[i, j] = a[i, j] - factor[k, i] * a[k, j]
-            rows[i] = rows[i] - factor[k, i] * rows[k]
-    for k in range(8):
-        done = jnp.where(lane < base + 8, rows[k] * (over[k] * jnp.sqrt(a[k, k])), 0.0)
-        inverse[base + k : base + k + 1, :] = done[0:1, :]
-    if panel == BLOCK // 8 - 1:
-        return
-    solved = [rows[k] * over[k] for k in range(8)]
-    for k in reversed(range(8)):
-        for i in range(k):
-            solved[i] = solved[i] - factor[i, k] * solved[k]
-    for r in range(base + 8, BLOCK, 8):
-        rest = m[r : r + 8, :]
-        terms = [jnp.broadcast_to(rest[:, base + k : base + k + 1], wide) * solved[k] for k in range(8)]
-        while len(terms) > 1:
-            terms = [x + y for x, y in zip(terms[::2], terms[1::2])]
-        m[r : r + 8, :] = jnp.where(within, 0.0, rest) - terms[0]
+                a[i, j] = a[i, j] - (factor[k, i] * a[k, j] + factor[k + 1, i] * a[k + 1, j])
+            rows[i] = rows[i] - (factor[k, i] * rows[k] + factor[k + 1, i] * rows[k + 1])
+    if panel < BLOCK // 8 - 1:
+        solved = [None] * 8
+        for k in range(0, 8, 2):
+            p, q, r = a[k, k] * over[k], a[k, k + 1] * over[k], a[k + 1, k + 1] * over[k]
+            solved[k] = r * rows[k] - q * rows[k + 1]
+            solved[k + 1] = p * rows[k + 1] - q * rows[k]
+        for k in (6, 4, 2):
+            for i in range(k):
+                solved[i] = solved[i] - (factor[i, k] * solved[k] + factor[i, k + 1] * solved[k + 1])
+        for r in range(base + 8, BLOCK, 8):
+            rest = m[r : r + 8, :]
+            terms = [jnp.broadcast_to(rest[:, base + k : base + k + 1], wide) * solved[k] for k in range(8)]
+            while len(terms) > 1:
+                terms = [x + y for x, y in zip(terms[::2], terms[1::2])]
+            m[r : r + 8, :] = jnp.where(within, 0.0, rest) - terms[0]
+    for k in range(0, 8, 2):
+        p, q = a[k, k], a[k, k + 1]
+        first = rows[k] * (scale[...] / jnp.sqrt(p))
+        second = (rows[k + 1] - rows[k] * (q / p)) * (scale[...] * jnp.sqrt(p * over[k]))
+        for j, done in ((base + k, first), (base + k + 1, second)):
+            inverse[j : j + 1, :] = jnp.where(lane < base + 8, done, 0.0)[0:1, :]
+
+
+def load_scaled(gram, m, scale):
+    value = gram[...]
+    rows = lax.broadcasted_iota(jnp.int32, value.shape, 0)
+    lanes = lax.broadcasted_iota(jnp.int32, value.shape, 1)
+    diagonal = jnp.sum(jnp.where(rows == lanes, value, 0.0), axis=0, keepdims=True)
+    over = 1.0 / jnp.broadcast_to(jnp.sum(diagonal, axis=1, keepdims=True), (8, BLOCK))
+    m[...] = value * over[0:1, :]
+    scale[...] = jnp.sqrt(over)
 
 
 def kernel(
     kernel_hbm, start, test, cutoff, subspace, projection,
-    buf, kf, khl, acc, m, inverse, loc, sib, lines, full, cloc, csib, clines, cfull, psend, precv,
+    buf, kf, khl, acc, m, inverse, scale, loc, sib, lines, full, cloc, csib, clines, cfull, psend, precv,
     ag_recv, ag_send, k_local, k_recv, k_send, ar_recv, ar_send, cr_recv, cr_send, p_recv, p_send,
 ):
     row, col = lax.axis_index("row"), lax.axis_index("col")
@@ -152,17 +149,18 @@
             src_ref=src, dst_ref=dst, send_sem=send, recv_sem=recv, device_id=to, device_id_type=MESH
         )
 
-    def block(par, s):
-        return buf.at[par, pl.ds(s * BLOCK, BLOCK)]
+    def block(par, s, count=1):
+        return buf.at[par, pl.ds(s * BLOCK, count * BLOCK)]
 
     def forward(par, s):
         for child, label in CHILDREN[s]:
             remote(
-                block(par, s), block(par, child), ag_send, ag_recv.at[par, child], neighbours[label]
+                block(par, s), block(par, child), ag_send, ag_recv.at[par, GROUP[child]], neighbours[label]
             ).start()
 
-    def arrived(par, s):
-        pltpu.make_async_copy(block(par, s), block(par, s), ag_recv.at[par, s]).wait()
+    def arrived(par, group):
+        whole = block(par, group, GROUP.count(group))
+        pltpu.make_async_copy(whole, whole, ag_recv.at[par, group]).wait()
 
     def columns(s, c):
         x, y, z = [lax.rem(p + RING - d, RING) for p, d in zip(here, ORDER[s])]
@@ -192,6 +190,9 @@
         khl[2 * BLOCK : 4 * BLOCK, lanes(c)] = (value - high.astype(jnp.float32)).astype(jnp.bfloat16)
 
     def multiply(par, c):
+        for group in sorted(set(GROUP[c * CHUNK : (c + 1) * CHUNK])):
+            if group >= INNER:
+                arrived(par, group)
         x = buf[par, pl.ds(c * CHUNK * BLOCK, CHUNK * BLOCK), :]
         high = x.astype(jnp.bfloat16)
         low = (x - high.astype(jnp.float32)).astype(jnp.bfloat16)
@@ -249,26 +250,30 @@
 
     def factor_panel(p):
         if p == 0:
-            m[...] = full_now[0][...]
-        eliminate(m, inverse, p)
+            load_scaled(full_now[0], m, scale)
+        eliminate(m, inverse, scale, p)
 
     full_now = [None]
 
-    def gather_and_multiply(par, tasks):
+    def gather_and_multiply(par, tasks, work, beside):
         forward(par, 0)
-        for s in range(SLOTS):
+        for s in range(INNER):
             if s:
                 arrived(par, s)
                 forward(par, s)
             for task in tasks.get(s, ()):
                 task()
+        for task in work:
+            task()
         value = acc[...]
         value = value[:, :BLOCK] + value[:, BLOCK:]
         value = value[: 2 * BLOCK] + value[2 * BLOCK :]
         psend[...] = value[BLOCK:]
         copy = remote(psend, precv.at[par], p_send, p_recv.at[par], sibling)
         copy.start()
-        whole = buf.at[par, pl.ds(BLOCK, (SLOTS - 1) * BLOCK)]
+        for task in beside:
+            task()
+        whole = block(par, 1, SLOTS - 1)
         pltpu.make_async_copy(whole, whole, ag_send).wait()
         copy.wait()
         return value[:BLOCK] + precv[par]
@@ -281,9 +286,11 @@
     tasks = {}
     for s in range(SLOTS):
         tasks.setdefault((s * 2) // 5, []).append(lambda s=s: start_kernel_copies(s))
+    work = []
     for c in range(SLOTS // CHUNK):
-        tasks.setdefault(35 + 4 * c, []).extend([lambda c=c: split_kernel(c), lambda c=c: multiply(0, c)])
-    image = gather_and_multiply(0, tasks)
+        into = tasks.setdefault((26, 28, 31, 33)[c], []) if c < 4 else work
+        into += [lambda c=c: split_kernel(c), lambda c=c: multiply(0, c)]
+    image = gather_and_multiply(0, tasks, work, [])
     buf[1, pl.ds(0, BLOCK), :] = image
     for c in range(SLOTS // CHUNK):
         given = kf.at[pl.ds(0, BLOCK), lanes(c)]
@@ -294,13 +301,15 @@
         stages = sum_stages(loc, sib.at[par], lines.at[par], full.at[par], ar_recv.at[par], ar_send)
         full_now[0] = full.at[par]
         tasks = {0: [lambda: local_gram(par), stages[0]]}
-        for at, stage in zip((0, 12, 26, 38, 44), stages[1:]):
+        for at, stage in zip((0, 6, 20, 35), stages[1:5]):
             tasks.setdefault(at, []).append(stage)
-        for p in range(16):
-            tasks.setdefault(45 + p, []).append(lambda p=p: factor_panel(p))
-        for c in range(SLOTS // CHUNK):
-            tasks.setdefault((c + 1) * CHUNK - 1, []).append(lambda c=c: multiply(par, c))
-        image = gather_and_multiply(par, tasks)
+        product = [lambda c=c: multiply(par, c) for c in range(SLOTS // CHUNK)]
+        panel = [lambda p=p: factor_panel(p) for p in range(16)]
+        for at, c in ((20, 0), (26, 1), (33, 2)):
+            tasks.setdefault(at, []).append(product[c])
+        work = [product[3], product[4], stages[5]]
+        work += panel[0:4] + [product[5]] + panel[4:8] + [product[6]] + panel[8:12] + [product[7]]
+        image = gather_and_multiply(par, tasks, work, panel[12:])
         buf[1 - par, pl.ds(0, BLOCK), :] = exact_dot(image, inverse[...], (((1,), (1,)), ((), ())))
         return carry
 
@@ -351,6 +360,7 @@
             pltpu.VMEM((4 * BLOCK, 2 * BLOCK), f32),
             pltpu.VMEM((BLOCK, BLOCK), f32),
             pltpu.VMEM((BLOCK, BLOCK), f32),
+            pltpu.VMEM((8, BLOCK), f32),
             pltpu.VMEM((BLOCK, BLOCK), f32),
             pltpu.VMEM((2, HALF, BLOCK), f32),
             pltpu.VMEM((2, 3, RING, HALF, BLOCK), f32),

time: 163 us -> 142 us (0.87)
  Pallas kernels: 158 us -> 138 us
    pallas_call x1, Pallas kernels: 158 us -> 138 us  [per_device(): pl.pallas_call(kernel, out_shape=(jax.ShapeDtypeStruct((BLOCK, BLOCK), f3...]
where the time goes in v2:
time: 142 us
  Pallas kernels  138 us (97%)
  local copies, waits for them, and re-layouts  3.04 us (2%)
    pallas_call x1, Pallas kernels, per_device(): pl.pallas_call(kernel, out_shape=(jax.ShapeDtypeStruct((BLOCK, BLOCK), f3...  138 us
    unnamed x2, local copies, waits for them, and re-layouts  3.04 us

profile of v2, /device:TPU:1, one launch (start us, length us, event | category | flops | bytes accessed | tf_op | source)
XLA Modules:
  0.0 141.9 jit_solution(10714593030376833068)
XLA Ops:
  1.3 137.5 %iterate.1 = (f32[128,128]{1,0:T(8,128)}, f32[128,256]{1,0:T(8,128)}) custom-call(f32[128,16384]{1,0:T(8,128)} %kernel_hbm.1, f32[128,128]{1,0:T(8,128)} %start.1, f32[128,256]{1,0:T(8,128)} %test.1, s32[1]{0:T(128)S(6)} %copy.8.cutoff), custom_call_target="tpu_custom_call" | custom-call | flops 8589934592 | bytes 16777216 | tf_op jit(solution)/shard_map/iterate/pallas_call | solution.py:348
  138.8 1.5 %copy.9 = f32[128,128]{1,0:T(8,128)} copy(f32[128,128]{1,0:T(8,128)} %get-tuple-element.4) | data formatting | bytes 131072
  140.3 1.6 %copy.10 = f32[128,256]{1,0:T(8,128)} copy(f32[128,256]{1,0:T(8,128)} %get-tuple-element.5) | data formatting | bytes 262144

commit v3 on v2

--- a/solution.py
+++ b/solution.py
@@ -14,6 +14,7 @@
 SLOTS = RING**3
 CHUNK = 8
 HALF = BLOCK // 2
+GROUPED = 32
 MESH = pl.DeviceIdType.MESH
 HIGHEST = lax.Precision.HIGHEST
 STEPS = [(axis, sign) for axis in range(3) for sign in (1, -1)]
@@ -60,8 +61,9 @@
     return r * (2.0 - x * r)
 
 
-def eliminate(m, inverse, scale, panel):
+def eliminate(m, inverse, scale, scaled, panel):
     base = 8 * panel
+    end = base // GROUPED * GROUPED + GROUPED
     wide = (8, BLOCK)
     lane = lax.broadcasted_iota(jnp.int32, wide, 1)
     within = (lane >= base) & (lane < base + 8)
@@ -81,7 +83,7 @@
             for j in range(i, 8):
                 a[i, j] = a[i, j] - (factor[k, i] * a[k, j] + factor[k + 1, i] * a[k + 1, j])
             rows[i] = rows[i] - (factor[k, i] * rows[k] + factor[k + 1, i] * rows[k + 1])
-    if panel < BLOCK // 8 - 1:
+    if base + 8 < end:
         solved = [None] * 8
         for k in range(0, 8, 2):
             p, q, r = a[k, k] * over[k], a[k, k + 1] * over[k], a[k + 1, k + 1] * over[k]
@@ -90,7 +92,7 @@
         for k in (6, 4, 2):
             for i in range(k):
                 solved[i] = solved[i] - (factor[i, k] * solved[k] + factor[i, k + 1] * solved[k + 1])
-        for r in range(base + 8, BLOCK, 8):
+        for r in range(base + 8, end, 8):
             rest = m[r : r + 8, :]
             terms = [jnp.broadcast_to(rest[:, base + k : base + k + 1], wide) * solved[k] for k in range(8)]
             while len(terms) > 1:
@@ -98,10 +100,18 @@
             m[r : r + 8, :] = jnp.where(within, 0.0, rest) - terms[0]
     for k in range(0, 8, 2):
         p, q = a[k, k], a[k, k + 1]
-        first = rows[k] * (scale[...] / jnp.sqrt(p))
-        second = (rows[k + 1] - rows[k] * (q / p)) * (scale[...] * jnp.sqrt(p * over[k]))
+        first = rows[k] * (1.0 / jnp.sqrt(p))
+        second = (rows[k + 1] - rows[k] * (q / p)) * jnp.sqrt(p * over[k])
         for j, done in ((base + k, first), (base + k + 1, second)):
-            inverse[j : j + 1, :] = jnp.where(lane < base + 8, done, 0.0)[0:1, :]
+            inverse[j : j + 1, :] = jnp.where(lane < base + 8, done * scale[...], 0.0)[0:1, :]
+            if end < BLOCK:
+                kept = (lane < base + 8) | (lane >= end)
+                scaled[j % GROUPED : j % GROUPED + 1, :] = jnp.where(kept, done, 0.0)[0:1, :]
+    if base + 8 == end and end < BLOCK:
+        done = scaled[...]
+        lanes = lax.broadcasted_iota(jnp.int32, (BLOCK - end, BLOCK), 1)
+        rest = jnp.where((lanes >= end - GROUPED) & (lanes < end), 0.0, m[end:, :])
+        m[end:, :] = rest - exact_dot(done.T[end:, :], done)
 
 
 def load_scaled(gram, m, scale):
@@ -115,8 +125,8 @@
 
 
 def kernel(
-    kernel_hbm, start, test, cutoff, subspace, projection,
-    buf, kf, khl, acc, m, inverse, scale, loc, sib, lines, full, cloc, csib, clines, cfull, psend, precv,
+    kernel_hbm, start, test, cutoff, image_out, inverse, kept_out,
+    buf, kf, khl, acc, m, scale, scaled, loc, sib, lines, full, cloc, csib, clines, cfull, psend, precv,
     ag_recv, ag_send, k_local, k_recv, k_send, ar_recv, ar_send, cr_recv, cr_send, p_recv, p_send,
 ):
     row, col = lax.axis_index("row"), lax.axis_index("col")
@@ -251,7 +261,7 @@
     def factor_panel(p):
         if p == 0:
             load_scaled(full_now[0], m, scale)
-        eliminate(m, inverse, scale, p)
+        eliminate(m, inverse, scale, scaled, p)
 
     full_now = [None]
 
@@ -333,11 +343,15 @@
         if p == 8:
             late[5]()
         factor_panel(p)
-    result = exact_dot(buf[par, pl.ds(0, BLOCK), :], inverse[...], (((1,), (1,)), ((), ())))
-    subspace[...] = result
+    image_out[...] = buf[par, pl.ds(0, BLOCK), :]
     keep = lax.broadcasted_iota(jnp.int32, (BLOCK, TEST), 0) < cutoff[0]
-    coefficients = exact_dot(inverse[...], cfull[...]) * jnp.where(keep, 1.0, 0.0)
-    projection[...] = exact_dot(result, coefficients)
+    kept_out[...] = exact_dot(inverse[...], cfull[...]) * jnp.where(keep, 1.0, 0.0)
+
+
+def project(image, inverse, kept, subspace, projection):
+    block = exact_dot(image[...], inverse[...], (((1,), (1,)), ((), ())))
+    subspace[...] = block
+    projection[...] = exact_dot(block, kept[...])
 
 
 def per_device(kernel_rows, start_block, test_kernel, cutoff):
@@ -345,22 +359,21 @@
     vmem = pl.BlockSpec(memory_space=pltpu.VMEM)
     dma = pltpu.SemaphoreType.DMA
     chunks = SLOTS // CHUNK
-    return pl.pallas_call(
+    narrow = jax.ShapeDtypeStruct((BLOCK, BLOCK), f32)
+    broad = jax.ShapeDtypeStruct((BLOCK, TEST), f32)
+    image, inverse, kept = pl.pallas_call(
         kernel,
-        out_shape=(
-            jax.ShapeDtypeStruct((BLOCK, BLOCK), f32),
-            jax.ShapeDtypeStruct((BLOCK, TEST), f32),
-        ),
+        out_shape=(narrow, narrow, broad),
         in_specs=[pl.BlockSpec(memory_space=pl.ANY), vmem, vmem, pl.BlockSpec(memory_space=pltpu.SMEM)],
-        out_specs=(vmem, vmem),
+        out_specs=(vmem, vmem, vmem),
         scratch_shapes=[
             pltpu.VMEM((2, SLOTS * BLOCK, BLOCK), f32),
             pltpu.VMEM((2 * BLOCK, SLOTS * BLOCK), f32),
             pltpu.VMEM((4 * BLOCK, SLOTS * BLOCK), jnp.bfloat16),
             pltpu.VMEM((4 * BLOCK, 2 * BLOCK), f32),
             pltpu.VMEM((BLOCK, BLOCK), f32),
-            pltpu.VMEM((BLOCK, BLOCK), f32),
             pltpu.VMEM((8, BLOCK), f32),
+            pltpu.VMEM((GROUPED, BLOCK), f32),
             pltpu.VMEM((BLOCK, BLOCK), f32),
             pltpu.VMEM((2, HALF, BLOCK), f32),
             pltpu.VMEM((2, 3, RING, HALF, BLOCK), f32),
@@ -391,6 +404,7 @@
         ),
         name="iterate",
     )(kernel_rows, start_block, test_kernel, cutoff)
+    return pl.pallas_call(project, out_shape=(narrow, broad), name="project")(image, inverse, kept)
 
 
 def solution(mesh):

time: 142 us -> 143 us (level)
  Pallas kernels: 138 us -> 142 us
  local copies, waits for them, and re-layouts: 3.04 us -> 0 us
    pallas_call x1 -> x2, Pallas kernels: 138 us -> 142 us  [the longest x1 140 us: per_device(): pl.pallas_call(kernel, out_shape=(narrow, narrow, broad), in_specs=[pl.Bl...]
    unnamed x2 -> x0, local copies, waits for them, and re-layouts: 3.04 us -> none
where the time goes in v3:
time: 143 us
  Pallas kernels  142 us (99%)
    pallas_call x1, Pallas kernels, per_device(): pl.pallas_call(kernel, out_shape=(narrow, narrow, broad), in_specs=[pl.Bl...  140 us

profile of v3, /device:TPU:1, one launch (start us, length us, event | category | flops | bytes accessed | tf_op | source)
XLA Modules:
  0.0 143.2 jit_solution(9783002014107628820)
XLA Ops:
  1.3 139.6 %iterate.1 = (f32[128,128]{1,0:T(8,128)}, f32[128,128]{1,0:T(8,128)}, f32[128,256]{1,0:T(8,128)}) custom-call(f32[128,16384]{1,0:T(8,128)} %kernel_hbm.1, f32[128,128]{1,0:T(8,128)} %start.1, f32[128,256]{1,0:T(8,128)} %test.1, s32[1]{0:T(128)S(6)} %copy.6.cutoff), custom_call_target="tpu_custom_call" | custom-call | flops 8589934592 | bytes 16777216 | tf_op jit(solution)/shard_map/iterate/pallas_call | solution.py:364
  140.9 2.3 %project.1 = (f32[128,128]{1,0:T(8,128)}, f32[128,256]{1,0:T(8,128)}) custom-call(f32[128,128]{1,0:T(8,128)} %get-tuple-element.5.image, f32[128,128]{1,0:T(8,128)} %get-tuple-element.6.inverse, f32[128,256]{1,0:T(8,128)} %get-tuple-element.7.kept), custom_call_target="tpu_custom_call" | custom-call | tf_op jit(solution)/shard_map/project/pallas_call | solution.py:407

commit v4 on v3

--- a/solution.py
+++ b/solution.py
@@ -14,7 +14,7 @@
 SLOTS = RING**3
 CHUNK = 8
 HALF = BLOCK // 2
-GROUPED = 32
+GROUPED = BLOCK
 MESH = pl.DeviceIdType.MESH
 HIGHEST = lax.Precision.HIGHEST
 STEPS = [(axis, sign) for axis in range(3) for sign in (1, -1)]
@@ -199,10 +199,12 @@
         khl[0 : 2 * BLOCK, lanes(c)] = high
         khl[2 * BLOCK : 4 * BLOCK, lanes(c)] = (value - high.astype(jnp.float32)).astype(jnp.bfloat16)
 
-    def multiply(par, c):
+    def leaves(par, c):
         for group in sorted(set(GROUP[c * CHUNK : (c + 1) * CHUNK])):
             if group >= INNER:
                 arrived(par, group)
+
+    def multiply(par, c):
         x = buf[par, pl.ds(c * CHUNK * BLOCK, CHUNK * BLOCK), :]
         high = x.astype(jnp.bfloat16)
         low = (x - high.astype(jnp.float32)).astype(jnp.bfloat16)
@@ -299,7 +301,7 @@
     work = []
     for c in range(SLOTS // CHUNK):
         into = tasks.setdefault((26, 28, 31, 33)[c], []) if c < 4 else work
-        into += [lambda c=c: split_kernel(c), lambda c=c: multiply(0, c)]
+        into += [lambda c=c: split_kernel(c), lambda c=c: leaves(0, c), lambda c=c: multiply(0, c)]
     image = gather_and_multiply(0, tasks, work, [])
     buf[1, pl.ds(0, BLOCK), :] = image
     for c in range(SLOTS // CHUNK):
@@ -317,9 +319,11 @@
         panel = [lambda p=p: factor_panel(p) for p in range(16)]
         for at, c in ((20, 0), (26, 1), (33, 2)):
             tasks.setdefault(at, []).append(product[c])
-        work = [product[3], product[4], stages[5]]
-        work += panel[0:4] + [product[5]] + panel[4:8] + [product[6]] + panel[8:12] + [product[7]]
-        image = gather_and_multiply(par, tasks, work, panel[12:])
+        work = [product[3], lambda: leaves(par, 4), product[4], stages[5]]
+        work += [lambda: leaves(par, 5), lambda: leaves(par, 6)]
+        work += [product[5]] + panel[0:4] + [product[6]] + panel[4:8]
+        work += [lambda: leaves(par, 7), product[7]]
+        image = gather_and_multiply(par, tasks, work, panel[8:])
         buf[1 - par, pl.ds(0, BLOCK), :] = exact_dot(image, inverse[...], (((1,), (1,)), ((), ())))
         return carry
 

time: 143 us -> 143 us (level)
  no operation moved by 1% of the time
where the time goes in v4:
time: 143 us; the launch traced here: 142 us
  Pallas kernels  141 us (99%)
    pallas_call x1, Pallas kernels, per_device(): pl.pallas_call(kernel, out_shape=(narrow, narrow, broad), in_specs=[pl.Bl...  139 us

profile of v4, /device:TPU:1, one launch (start us, length us, event | category | flops | bytes accessed | tf_op | source)
XLA Modules:
  0.0 142.4 jit_solution(16133541193823601810)
XLA Ops:
  1.3 138.8 %iterate.1 = (f32[128,128]{1,0:T(8,128)}, f32[128,128]{1,0:T(8,128)}, f32[128,256]{1,0:T(8,128)}) custom-call(f32[128,16384]{1,0:T(8,128)} %kernel_hbm.1, f32[128,128]{1,0:T(8,128)} %start.1, f32[128,256]{1,0:T(8,128)} %test.1, s32[1]{0:T(128)S(6)} %copy.6.cutoff), custom_call_target="tpu_custom_call" | custom-call | flops 8589934592 | bytes 16777216 | tf_op jit(solution)/shard_map/iterate/pallas_call | solution.py:368
  140.1 2.3 %project.1 = (f32[128,128]{1,0:T(8,128)}, f32[128,256]{1,0:T(8,128)}) custom-call(f32[128,128]{1,0:T(8,128)} %get-tuple-element.5.image, f32[128,128]{1,0:T(8,128)} %get-tuple-element.6.inverse, f32[128,256]{1,0:T(8,128)} %get-tuple-element.7.kept), custom_call_target="tpu_custom_call" | custom-call | tf_op jit(solution)/shard_map/project/pallas_call | solution.py:411

commit v5 on v4

--- a/solution.py
+++ b/solution.py
@@ -13,7 +13,8 @@
 RING = 4
 SLOTS = RING**3
 CHUNK = 8
-HALF = BLOCK // 2
+TEAM = 2 * RING
+PIECE = BLOCK // TEAM
 GROUPED = BLOCK
 MESH = pl.DeviceIdType.MESH
 HIGHEST = lax.Precision.HIGHEST
@@ -126,7 +127,7 @@
 
 def kernel(
     kernel_hbm, start, test, cutoff, image_out, inverse, kept_out,
-    buf, kf, khl, acc, m, scale, scaled, loc, sib, lines, full, cloc, csib, clines, cfull, psend, precv,
+    buf, kf, khl, acc, m, scale, scaled, loc, pieces, lines, full, cloc, cpieces, clines, cfull, psend, precv,
     ag_recv, ag_send, k_local, k_recv, k_send, ar_recv, ar_send, cr_recv, cr_send, p_recv, p_send,
 ):
     row, col = lax.axis_index("row"), lax.axis_index("col")
@@ -149,7 +150,8 @@
     neighbours = [moved(axis, 1 if sign > 0 else RING - 1) for axis, sign in STEPS]
 
     barrier = pltpu.get_barrier_semaphore()
-    greet = [moved(axis, by) for axis in range(3) for by in (1, 2, 3)] + [sibling]
+    greet = [moved(axis, by) for axis in range(3) for by in (1, 2, 3)]
+    greet += [device(lax.rem(here[0] + by, RING), here[1], here[2], 1 - core) for by in range(RING)]
     for other in greet:
         pl.semaphore_signal(barrier, inc=1, device_id=other, device_id_type=MESH)
     pl.semaphore_wait(barrier, len(greet))
@@ -216,10 +218,15 @@
         else:
             acc[...] += term
 
-    def sum_stages(loc, sib, lines, full, recv, send):
-        kept = pl.ds(pl.multiple_of(core * HALF, HALF), HALF)
-        given = pl.ds(pl.multiple_of((1 - core) * HALF, HALF), HALF)
+    def sum_stages(loc, pieces, lines, full, recv, send):
+        me = here[0] * 2 + core
         sent = []
+
+        def member(by):
+            return lax.rem(me + by, TEAM)
+
+        def part(e):
+            return pl.ds(pl.multiple_of(e * PIECE, PIECE), PIECE)
 
         def start(src, dst, index, to):
             copy = remote(src, dst, send.at[index], recv.at[index], to)
@@ -229,36 +236,49 @@
         def wait(ref, index):
             pltpu.make_async_copy(ref, ref, recv.at[index]).wait()
 
+        def to_team(source, target, first):
+            for by in range(1, TEAM):
+                e = member(by)
+                start(source(e), target(me), first + by - 1, device(lax.div(e, 2), here[1], here[2], lax.rem(e, 2)))
+
+        def from_team(target, first):
+            for by in range(1, TEAM):
+                wait(target(member(TEAM - by)), first + by - 1)
+
         def to_line(axis, value):
-            mine = lines.at[axis, here[axis]]
+            mine = lines.at[axis - 1, here[axis]]
             mine[...] = value
             for by in (1, 2, 3):
-                start(mine, mine, 1 + 3 * axis + by - 1, moved(axis, by))
+                start(mine, mine, 3 + 3 * axis + by, moved(axis, by))
 
         def from_line(axis):
             for by in (1, 2, 3):
-                wait(lines.at[axis, lax.rem(here[axis] + RING - by, RING)], 1 + 3 * axis + by - 1)
-            return (lines[axis, 0] + lines[axis, 1]) + (lines[axis, 2] + lines[axis, 3])
-
-        def first():
-            start(loc.at[given], sib, 0, sibling)
-
-        def second():
-            wait(sib, 0)
-            to_line(0, loc[kept, :] + sib[...])
-
-        def fifth():
-            full[kept, :] = from_line(2)
-            start(full.at[kept], full.at[kept], 10, sibling)
-
-        def last():
-            wait(full.at[given], 10)
+                wait(lines.at[axis - 1, lax.rem(here[axis] + RING - by, RING)], 3 + 3 * axis + by)
+            got = [lines[axis - 1, p] for p in range(RING)]
+            return (got[0] + got[1]) + (got[2] + got[3])
+
+        def scatter():
+            to_team(lambda e: loc.at[part(e)], lambda e: pieces.at[e], 0)
+            pieces[me] = loc[part(me), :]
+
+        def along_y():
+            from_team(lambda e: pieces.at[e], 0)
+            got = [pieces[e] for e in range(TEAM)]
+            to_line(1, ((got[0] + got[1]) + (got[2] + got[3])) + ((got[4] + got[5]) + (got[6] + got[7])))
+
+        def along_z():
+            to_line(2, from_line(1))
+
+        def gather():
+            full[part(me), :] = from_line(2)
+            to_team(lambda e: full.at[part(me)], lambda e: full.at[part(e)], 13)
+
+        def finish():
+            from_team(lambda e: full.at[part(e)], 13)
             for copy in sent:
                 copy.wait_send()
 
-        return [
-            first, second, lambda: to_line(1, from_line(0)), lambda: to_line(2, from_line(1)), fifth, last
-        ]
+        return [scatter, along_y, along_z, gather, finish]
 
     def factor_panel(p):
         if p == 0:
@@ -310,42 +330,41 @@
 
     def step(t, carry):
         par = lax.rem(t, 2)
-        stages = sum_stages(loc, sib.at[par], lines.at[par], full.at[par], ar_recv.at[par], ar_send)
+        stages = sum_stages(loc, pieces.at[par], lines.at[par], full.at[par], ar_recv.at[par], ar_send)
         full_now[0] = full.at[par]
         tasks = {0: [lambda: local_gram(par), stages[0]]}
-        for at, stage in zip((0, 6, 20, 35), stages[1:5]):
+        for at, stage in zip((0, 6, 18, 28), stages[1:]):
             tasks.setdefault(at, []).append(stage)
         product = [lambda c=c: multiply(par, c) for c in range(SLOTS // CHUNK)]
         panel = [lambda p=p: factor_panel(p) for p in range(16)]
-        for at, c in ((20, 0), (26, 1), (33, 2)):
-            tasks.setdefault(at, []).append(product[c])
-        work = [product[3], lambda: leaves(par, 4), product[4], stages[5]]
-        work += [lambda: leaves(par, 5), lambda: leaves(par, 6)]
-        work += [product[5]] + panel[0:4] + [product[6]] + panel[4:8]
+        for at, task in [(20, product[0]), (26, product[1])] + [(28 + p, panel[p]) for p in range(8)]:
+            tasks.setdefault(at, []).append(task)
+        work = [product[2], product[3], lambda: leaves(par, 4), product[4]]
+        work += [lambda: leaves(par, 5), lambda: leaves(par, 6), product[5], product[6]] + panel[8:12]
         work += [lambda: leaves(par, 7), product[7]]
-        image = gather_and_multiply(par, tasks, work, panel[8:])
+        image = gather_and_multiply(par, tasks, work, panel[12:])
         buf[1 - par, pl.ds(0, BLOCK), :] = exact_dot(image, inverse[...], (((1,), (1,)), ((), ())))
         return carry
 
     lax.fori_loop(1, ITERATIONS, step, 0)
 
     par = ITERATIONS % 2
-    stages = sum_stages(loc, sib.at[par], lines.at[par], full.at[par], ar_recv.at[par], ar_send)
-    late = sum_stages(cloc, csib, clines, cfull, cr_recv, cr_send)
+    stages = sum_stages(loc, pieces.at[par], lines.at[par], full.at[par], ar_recv.at[par], ar_send)
+    late = sum_stages(cloc, cpieces, clines, cfull, cr_recv, cr_send)
     full_now[0] = full.at[par]
     local_gram(par)
     stages[0]()
     last = buf[par, pl.ds(0, BLOCK), :]
     cloc[...] = exact_dot(last.T, test[...])
     stages[1]()
-    for one, two in zip(late[:4], stages[2:]):
+    for one, two in zip(late[:3], stages[2:]):
         one()
         two()
     for p in range(16):
         if p == 4:
+            late[3]()
+        if p == 10:
             late[4]()
-        if p == 8:
-            late[5]()
         factor_panel(p)
     image_out[...] = buf[par, pl.ds(0, BLOCK), :]
     keep = lax.broadcasted_iota(jnp.int32, (BLOCK, TEST), 0) < cutoff[0]
@@ -379,12 +398,12 @@
             pltpu.VMEM((8, BLOCK), f32),
             pltpu.VMEM((GROUPED, BLOCK), f32),
             pltpu.VMEM((BLOCK, BLOCK), f32),
-            pltpu.VMEM((2, HALF, BLOCK), f32),
-            pltpu.VMEM((2, 3, RING, HALF, BLOCK), f32),
+            pltpu.VMEM((2, TEAM, PIECE, BLOCK), f32),
+            pltpu.VMEM((2, 2, RING, PIECE, BLOCK), f32),
             pltpu.VMEM((2, BLOCK, BLOCK), f32),
             pltpu.VMEM((BLOCK, TEST), f32),
-            pltpu.VMEM((HALF, TEST), f32),
-            pltpu.VMEM((3, RING, HALF, TEST), f32),
+            pltpu.VMEM((TEAM, PIECE, TEST), f32),
+            pltpu.VMEM((2, RING, PIECE, TEST), f32),
             pltpu.VMEM((BLOCK, TEST), f32),
             pltpu.VMEM((BLOCK, BLOCK), f32),
             pltpu.VMEM((2, BLOCK, BLOCK), f32),
@@ -393,10 +412,10 @@
             dma((chunks,)),
             dma((chunks,)),
             dma((chunks,)),
-            dma((2, 11)),
-            dma((11,)),
-            dma((11,)),
-            dma((11,)),
+            dma((2, 20)),
+            dma((20,)),
+            dma((20,)),
+            dma((20,)),
             dma((2,)),
             dma,
         ],

time: 143 us -> 146 us (1.021)
  Pallas kernels: 141 us -> 144 us
    pallas_call x1, Pallas kernels: 139 us -> 142 us  [per_device(): pl.pallas_call(kernel, out_shape=(narrow, narrow, broad), in_specs=[pl.Bl...]
where the time goes in v5:
time: 146 us; the launch traced here: 145 us
  Pallas kernels  144 us (99%)
    pallas_call x1, Pallas kernels, per_device(): pl.pallas_call(kernel, out_shape=(narrow, narrow, broad), in_specs=[pl.Bl...  142 us

profile of v5, /device:TPU:1, one launch (start us, length us, event | category | flops | bytes accessed | tf_op | source)
XLA Modules:
  0.0 145.5 jit_solution(2490234994539429103)
XLA Ops:
  1.3 141.9 %iterate.1 = (f32[128,128]{1,0:T(8,128)}, f32[128,128]{1,0:T(8,128)}, f32[128,256]{1,0:T(8,128)}) custom-call(f32[128,16384]{1,0:T(8,128)} %kernel_hbm.1, f32[128,128]{1,0:T(8,128)} %start.1, f32[128,256]{1,0:T(8,128)} %test.1, s32[1]{0:T(128)S(6)} %copy.6.cutoff), custom_call_target="tpu_custom_call" | custom-call | flops 8589934592 | bytes 16777216 | tf_op jit(solution)/shard_map/iterate/pallas_call | solution.py:387
  143.2 2.3 %project.1 = (f32[128,128]{1,0:T(8,128)}, f32[128,256]{1,0:T(8,128)}) custom-call(f32[128,128]{1,0:T(8,128)} %get-tuple-element.5.image, f32[128,128]{1,0:T(8,128)} %get-tuple-element.6.inverse, f32[128,256]{1,0:T(8,128)} %get-tuple-element.7.kept), custom_call_target="tpu_custom_call" | custom-call | tf_op jit(solution)/shard_map/project/pallas_call | solution.py:430

commit v6 on v5

--- a/solution.py
+++ b/solution.py
@@ -13,41 +13,35 @@
 RING = 4
 SLOTS = RING**3
 CHUNK = 8
-TEAM = 2 * RING
+TEAM = RING * RING
+LINE = 2 * RING
 PIECE = BLOCK // TEAM
 GROUPED = BLOCK
 MESH = pl.DeviceIdType.MESH
 HIGHEST = lax.Precision.HIGHEST
-STEPS = [(axis, sign) for axis in range(3) for sign in (1, -1)]
-
 
 TREE = (
-    0, 75, 10, 96, 26, 23, 289, 51, 95, 168, 295, 32, 16, 81, 102, 307,
-    122, 363, 47, 192, 58, 369, 71, 126, 199, 177, 332, 343, 41, 376, 355, 267,
-    138, 208, 247, 184, 119, 314, 379, 304, 320, 191, 108, 88, 339, 216, 146, 215,
-    152, 65, 162, 224, 351, 277, 329, 132, 274, 243, 230, 259, 287, 234, 256, 159,
+    0, 768, 3072, 64, 448, 256, 1088, 1024, 3840, 832, 320, 961, 708, 2050, 3138, 4033,
+    1732, 3333, 131, 1223, 3592, 1287, 3913, 1354, 2182, 585, 2317, 1995, 1158, 652, 2768, 3218,
+    192, 3264, 513, 1793, 1862, 907, 2126, 2829, 394, 1491, 3791, 3983, 2259, 3409, 2580, 1557,
+    3670, 3537, 1431, 1625, 2902, 2456, 2968, 2522, 3035, 2394, 3741, 1948, 2718, 1693, 2650, 3487,
 )
-
-
-def spanning_tree():
-    order = [(code // 96, code // 24 % 4, code // 6 % 4) for code in TREE]
-    slot = {d: s for s, d in enumerate(order)}
-    children = [[] for _ in order]
-    height = [0] * len(order)
-    depth = lambda s: sum(min(c, RING - c) for c in order[s])
-    for s in sorted(range(1, len(order)), key=depth, reverse=True):
-        axis, sign = STEPS[TREE[s] % 6]
-        before = list(order[s])
-        before[axis] = (before[axis] - sign) % RING
-        parent = slot[tuple(before)]
-        children[parent].append((s, TREE[s] % 6))
-        height[parent] = max(height[parent], height[s] + 1)
+ORDER = [(code // 1024, code // 256 % 4, code // 64 % 4) for code in TREE]
+PARENT = [code % 64 for code in TREE]
+
+
+def passed_on():
+    children = [[] for _ in TREE]
+    height = [0] * SLOTS
+    for s in reversed(range(1, SLOTS)):
+        children[PARENT[s]].append(s)
+        height[PARENT[s]] = max(height[PARENT[s]], height[s] + 1)
     for found in children:
-        found.sort(key=lambda child: -height[child[0]])
-    return order, children
-
-
-ORDER, CHILDREN = spanning_tree()
+        found.sort(key=lambda s: -height[s])
+    return children
+
+
+CHILDREN = passed_on()
 INNER = sum(1 for found in CHILDREN if found)
 GROUP = [s if s < INNER else max(INNER, s // CHUNK * CHUNK) for s in range(SLOTS)]
 
@@ -115,8 +109,7 @@
         m[end:, :] = rest - exact_dot(done.T[end:, :], done)
 
 
-def load_scaled(gram, m, scale):
-    value = gram[...]
+def load_scaled(value, m, scale):
     rows = lax.broadcasted_iota(jnp.int32, value.shape, 0)
     lanes = lax.broadcasted_iota(jnp.int32, value.shape, 1)
     diagonal = jnp.sum(jnp.where(rows == lanes, value, 0.0), axis=0, keepdims=True)
@@ -141,17 +134,20 @@
     def device(x, y, z, c):
         return (z * 2 + lax.rem(x, 2), (y * 2 + lax.div(x, 2)) * 2 + c)
 
-    def moved(axis, by):
-        place = list(here)
-        place[axis] = lax.rem(place[axis] + by, RING)
-        return device(*place, core)
+    def moved(by, core=core):
+        return device(*[lax.rem(p + b, RING) for p, b in zip(here, by)], core)
+
+    def hop(s):
+        return tuple((a - b) % RING for a, b in zip(ORDER[s], ORDER[PARENT[s]]))
 
     sibling = device(*here, 1 - core)
-    neighbours = [moved(axis, 1 if sign > 0 else RING - 1) for axis, sign in STEPS]
+    near = {hop(s) for s in range(1, SLOTS)}
+    near |= {tuple(-b % RING for b in by) for by in near}
+    near |= {(x, y, 0) for x in range(RING) for y in range(RING)} | {(0, 0, z) for z in range(RING)}
+    greet = [moved(by) for by in sorted(near - {(0, 0, 0)})]
+    greet += [moved((0, 0, z), 1 - core) for z in range(RING)]
 
     barrier = pltpu.get_barrier_semaphore()
-    greet = [moved(axis, by) for axis in range(3) for by in (1, 2, 3)]
-    greet += [device(lax.rem(here[0] + by, RING), here[1], here[2], 1 - core) for by in range(RING)]
     for other in greet:
         pl.semaphore_signal(barrier, inc=1, device_id=other, device_id_type=MESH)
     pl.semaphore_wait(barrier, len(greet))
@@ -165,9 +161,9 @@
         return buf.at[par, pl.ds(s * BLOCK, count * BLOCK)]
 
     def forward(par, s):
-        for child, label in CHILDREN[s]:
+        for child in CHILDREN[s]:
             remote(
-                block(par, s), block(par, child), ag_send, ag_recv.at[par, GROUP[child]], neighbours[label]
+                block(par, s), block(par, child), ag_send, ag_recv.at[par, GROUP[child]], moved(hop(child))
             ).start()
 
     def arrived(par, group):
@@ -218,71 +214,59 @@
         else:
             acc[...] += term
 
-    def sum_stages(loc, pieces, lines, full, recv, send):
-        me = here[0] * 2 + core
-        sent = []
-
-        def member(by):
-            return lax.rem(me + by, TEAM)
+    def sum_stages(loc, pieces, line, full, recv, send):
+        me = here[0] * RING + here[1]
+        spot = here[2] * 2 + core
 
         def part(e):
             return pl.ds(pl.multiple_of(e * PIECE, PIECE), PIECE)
 
-        def start(src, dst, index, to):
-            copy = remote(src, dst, send.at[index], recv.at[index], to)
-            copy.start()
-            sent.append(copy)
-
-        def wait(ref, index):
-            pltpu.make_async_copy(ref, ref, recv.at[index]).wait()
-
-        def to_team(source, target, first):
+        def to_team(source, target, stage):
             for by in range(1, TEAM):
-                e = member(by)
-                start(source(e), target(me), first + by - 1, device(lax.div(e, 2), here[1], here[2], lax.rem(e, 2)))
-
-        def from_team(target, first):
-            for by in range(1, TEAM):
-                wait(target(member(TEAM - by)), first + by - 1)
-
-        def to_line(axis, value):
-            mine = lines.at[axis - 1, here[axis]]
-            mine[...] = value
-            for by in (1, 2, 3):
-                start(mine, mine, 3 + 3 * axis + by, moved(axis, by))
-
-        def from_line(axis):
-            for by in (1, 2, 3):
-                wait(lines.at[axis - 1, lax.rem(here[axis] + RING - by, RING)], 3 + 3 * axis + by)
-            got = [lines[axis - 1, p] for p in range(RING)]
-            return (got[0] + got[1]) + (got[2] + got[3])
+                e = lax.rem(me + by, TEAM)
+                to = device(lax.div(e, RING), lax.rem(e, RING), here[2], core)
+                remote(source(e), target.at[by - 1], send.at[stage], recv.at[stage], to).start()
+
+        def await_all(target, count, semaphore):
+            whole = target.at[pl.ds(0, count)]
+            pltpu.make_async_copy(whole, whole, semaphore).wait()
+
+        def tree_sum(got):
+            while len(got) > 1:
+                got = [x + y for x, y in zip(got[::2], got[1::2])]
+            return got[0]
 
         def scatter():
-            to_team(lambda e: loc.at[part(e)], lambda e: pieces.at[e], 0)
-            pieces[me] = loc[part(me), :]
-
-        def along_y():
-            from_team(lambda e: pieces.at[e], 0)
-            got = [pieces[e] for e in range(TEAM)]
-            to_line(1, ((got[0] + got[1]) + (got[2] + got[3])) + ((got[4] + got[5]) + (got[6] + got[7])))
-
-        def along_z():
-            to_line(2, from_line(1))
+            to_team(lambda e: loc.at[part(e)], pieces, 0)
+
+        def exchange():
+            await_all(pieces, TEAM - 1, recv.at[0])
+            line[LINE - 1] = tree_sum([pieces[k] for k in range(TEAM - 1)] + [loc[part(me), :]])
+            for by in range(1, LINE):
+                f = lax.rem(spot + by, LINE)
+                to = device(here[0], here[1], lax.div(f, 2), lax.rem(f, 2))
+                remote(line.at[LINE - 1], line.at[by - 1], send.at[1], recv.at[1], to).start()
 
         def gather():
-            full[part(me), :] = from_line(2)
-            to_team(lambda e: full.at[part(me)], lambda e: full.at[part(e)], 13)
+            await_all(line, LINE - 1, recv.at[1])
+            full[TEAM - 1] = tree_sum([line[lax.rem(spot - f + 2 * LINE - 1, LINE)] for f in range(LINE)])
+            to_team(lambda e: full.at[TEAM - 1], full, 2)
 
         def finish():
-            from_team(lambda e: full.at[part(e)], 13)
-            for copy in sent:
-                copy.wait_send()
-
-        return [scatter, along_y, along_z, gather, finish]
+            await_all(full, TEAM - 1, recv.at[2])
+            await_all(pieces, TEAM - 1, send.at[0])
+            await_all(line, LINE - 1, send.at[1])
+            await_all(full, TEAM - 1, send.at[2])
+
+        return [scatter, exchange, gather, finish]
+
+    def whole_sum(full):
+        me = here[0] * RING + here[1]
+        return jnp.concatenate([full[lax.rem(me - e + 2 * TEAM - 1, TEAM)] for e in range(TEAM)], axis=0)
 
     def factor_panel(p):
         if p == 0:
-            load_scaled(full_now[0], m, scale)
+            load_scaled(whole_sum(full_now[0]), m, scale)
         eliminate(m, inverse, scale, scaled, p)
 
     full_now = [None]
@@ -320,7 +304,7 @@
         tasks.setdefault((s * 2) // 5, []).append(lambda s=s: start_kernel_copies(s))
     work = []
     for c in range(SLOTS // CHUNK):
-        into = tasks.setdefault((26, 28, 31, 33)[c], []) if c < 4 else work
+        into = tasks.setdefault((25, 29)[c], []) if c < 2 else work
         into += [lambda c=c: split_kernel(c), lambda c=c: leaves(0, c), lambda c=c: multiply(0, c)]
     image = gather_and_multiply(0, tasks, work, [])
     buf[1, pl.ds(0, BLOCK), :] = image
@@ -333,15 +317,15 @@
         stages = sum_stages(loc, pieces.at[par], lines.at[par], full.at[par], ar_recv.at[par], ar_send)
         full_now[0] = full.at[par]
         tasks = {0: [lambda: local_gram(par), stages[0]]}
-        for at, stage in zip((0, 6, 18, 28), stages[1:]):
+        for at, stage in zip((5, 13), stages[1:3]):
             tasks.setdefault(at, []).append(stage)
         product = [lambda c=c: multiply(par, c) for c in range(SLOTS // CHUNK)]
         panel = [lambda p=p: factor_panel(p) for p in range(16)]
-        for at, task in [(20, product[0]), (26, product[1])] + [(28 + p, panel[p]) for p in range(8)]:
-            tasks.setdefault(at, []).append(task)
-        work = [product[2], product[3], lambda: leaves(par, 4), product[4]]
-        work += [lambda: leaves(par, 5), lambda: leaves(par, 6), product[5], product[6]] + panel[8:12]
-        work += [lambda: leaves(par, 7), product[7]]
+        for at, c in ((20, 0), (25, 1), (29, 2)):
+            tasks.setdefault(at, []).append(product[c])
+        work = [product[3], stages[3]] + panel[0:4]
+        work += [lambda: leaves(par, 4), lambda: leaves(par, 5), product[4], product[5]] + panel[4:8]
+        work += [lambda: leaves(par, 6), product[6]] + panel[8:12] + [lambda: leaves(par, 7), product[7]]
         image = gather_and_multiply(par, tasks, work, panel[12:])
         buf[1 - par, pl.ds(0, BLOCK), :] = exact_dot(image, inverse[...], (((1,), (1,)), ((), ())))
         return carry
@@ -356,19 +340,19 @@
     stages[0]()
     last = buf[par, pl.ds(0, BLOCK), :]
     cloc[...] = exact_dot(last.T, test[...])
+    late[0]()
     stages[1]()
-    for one, two in zip(late[:3], stages[2:]):
-        one()
-        two()
+    late[1]()
+    stages[2]()
+    late[2]()
+    stages[3]()
     for p in range(16):
-        if p == 4:
+        if p == 8:
             late[3]()
-        if p == 10:
-            late[4]()
         factor_panel(p)
     image_out[...] = buf[par, pl.ds(0, BLOCK), :]
     keep = lax.broadcasted_iota(jnp.int32, (BLOCK, TEST), 0) < cutoff[0]
-    kept_out[...] = exact_dot(inverse[...], cfull[...]) * jnp.where(keep, 1.0, 0.0)
+    kept_out[...] = exact_dot(inverse[...], whole_sum(cfull)) * jnp.where(keep, 1.0, 0.0)
 
 
 def project(image, inverse, kept, subspace, projection):
@@ -399,12 +383,12 @@
             pltpu.VMEM((GROUPED, BLOCK), f32),
             pltpu.VMEM((BLOCK, BLOCK), f32),
             pltpu.VMEM((2, TEAM, PIECE, BLOCK), f32),
-            pltpu.VMEM((2, 2, RING, PIECE, BLOCK), f32),
-            pltpu.VMEM((2, BLOCK, BLOCK), f32),
+            pltpu.VMEM((2, LINE, PIECE, BLOCK), f32),
+            pltpu.VMEM((2, TEAM, PIECE, BLOCK), f32),
             pltpu.VMEM((BLOCK, TEST), f32),
             pltpu.VMEM((TEAM, PIECE, TEST), f32),
-            pltpu.VMEM((2, RING, PIECE, TEST), f32),
-            pltpu.VMEM((BLOCK, TEST), f32),
+            pltpu.VMEM((LINE, PIECE, TEST), f32),
+            pltpu.VMEM((TEAM, PIECE, TEST), f32),
             pltpu.VMEM((BLOCK, BLOCK), f32),
             pltpu.VMEM((2, BLOCK, BLOCK), f32),
             dma((2, SLOTS)),
@@ -412,10 +396,10 @@
             dma((chunks,)),
             dma((chunks,)),
             dma((chunks,)),
-            dma((2, 20)),
-            dma((20,)),
-            dma((20,)),
-            dma((20,)),
+            dma((2, 3)),
+            dma((3,)),
+            dma((3,)),
+            dma((3,)),
             dma((2,)),
             dma,
         ],

time: 146 us -> 135 us (0.925)
  Pallas kernels: 144 us -> 134 us
    pallas_call x1, Pallas kernels: 142 us -> 131 us  [per_device(): pl.pallas_call(kernel, out_shape=(narrow, narrow, broad), in_specs=[pl.Bl...]
where the time goes in v6:
time: 135 us
  Pallas kernels  134 us (99%)
    pallas_call x1, Pallas kernels, per_device(): pl.pallas_call(kernel, out_shape=(narrow, narrow, broad), in_specs=[pl.Bl...  131 us

profile of v6, /device:TPU:1, one launch (start us, length us, event | category | flops | bytes accessed | tf_op | source)
XLA Modules:
  0.0 135.0 jit_solution(4146618040166491895)
XLA Ops:
  1.3 131.4 %iterate.1 = (f32[128,128]{1,0:T(8,128)}, f32[128,128]{1,0:T(8,128)}, f32[128,256]{1,0:T(8,128)}) custom-call(f32[128,16384]{1,0:T(8,128)} %kernel_hbm.1, f32[128,128]{1,0:T(8,128)} %start.1, f32[128,256]{1,0:T(8,128)} %test.1, s32[1]{0:T(128)S(6)} %copy.6.cutoff), custom_call_target="tpu_custom_call" | custom-call | flops 8589934592 | bytes 16777216 | tf_op jit(solution)/shard_map/iterate/pallas_call | solution.py:371
  132.7 2.3 %project.1 = (f32[128,128]{1,0:T(8,128)}, f32[128,256]{1,0:T(8,128)}) custom-call(f32[128,128]{1,0:T(8,128)} %get-tuple-element.5.image, f32[128,128]{1,0:T(8,128)} %get-tuple-element.6.inverse, f32[128,256]{1,0:T(8,128)} %get-tuple-element.7.kept), custom_call_target="tpu_custom_call" | custom-call | tf_op jit(solution)/shard_map/project/pallas_call | solution.py:414

commit v7 on v6

--- a/solution.py
+++ b/solution.py
@@ -21,10 +21,10 @@
 HIGHEST = lax.Precision.HIGHEST
 
 TREE = (
-    0, 768, 3072, 64, 448, 256, 1088, 1024, 3840, 832, 320, 961, 708, 2050, 3138, 4033,
-    1732, 3333, 131, 1223, 3592, 1287, 3913, 1354, 2182, 585, 2317, 1995, 1158, 652, 2768, 3218,
-    192, 3264, 513, 1793, 1862, 907, 2126, 2829, 394, 1491, 3791, 3983, 2259, 3409, 2580, 1557,
-    3670, 3537, 1431, 1625, 2902, 2456, 2968, 2522, 3035, 2394, 3741, 1948, 2718, 1693, 2650, 3487,
+    0, 3072, 192, 64, 1024, 960, 320, 256, 768, 1088, 3264, 2049, 3841, 3139, 1474, 130,
+    835, 3393, 1989, 1796, 4037, 582, 3335, 1161, 520, 2315, 3210, 3916, 2125, 2385, 1742, 3988,
+    1220, 455, 390, 1287, 709, 1353, 2510, 2251, 912, 3026, 1875, 1621, 2827, 3669, 1935, 661,
+    1431, 3542, 1555, 3608, 2585, 3796, 2782, 2907, 3482, 1694, 2204, 2653, 2718, 2461, 2975, 3743,
 )
 ORDER = [(code // 1024, code // 256 % 4, code // 64 % 4) for code in TREE]
 PARENT = [code % 64 for code in TREE]
@@ -304,7 +304,7 @@
         tasks.setdefault((s * 2) // 5, []).append(lambda s=s: start_kernel_copies(s))
     work = []
     for c in range(SLOTS // CHUNK):
-        into = tasks.setdefault((25, 29)[c], []) if c < 2 else work
+        into = tasks.setdefault((24, 30)[c], []) if c < 2 else work
         into += [lambda c=c: split_kernel(c), lambda c=c: leaves(0, c), lambda c=c: multiply(0, c)]
     image = gather_and_multiply(0, tasks, work, [])
     buf[1, pl.ds(0, BLOCK), :] = image
@@ -317,16 +317,15 @@
         stages = sum_stages(loc, pieces.at[par], lines.at[par], full.at[par], ar_recv.at[par], ar_send)
         full_now[0] = full.at[par]
         tasks = {0: [lambda: local_gram(par), stages[0]]}
-        for at, stage in zip((5, 13), stages[1:3]):
+        for at, stage in zip((8, 23), stages[1:3]):
             tasks.setdefault(at, []).append(stage)
         product = [lambda c=c: multiply(par, c) for c in range(SLOTS // CHUNK)]
         panel = [lambda p=p: factor_panel(p) for p in range(16)]
-        for at, c in ((20, 0), (25, 1), (29, 2)):
+        for at, c in ((24, 0), (28, 1), (30, 2)):
             tasks.setdefault(at, []).append(product[c])
-        work = [product[3], stages[3]] + panel[0:4]
-        work += [lambda: leaves(par, 4), lambda: leaves(par, 5), product[4], product[5]] + panel[4:8]
-        work += [lambda: leaves(par, 6), product[6]] + panel[8:12] + [lambda: leaves(par, 7), product[7]]
-        image = gather_and_multiply(par, tasks, work, panel[12:])
+        work = [product[3], lambda: leaves(par, 4), product[4], lambda: leaves(par, 5), product[5], stages[3]]
+        work += panel[0:4] + [lambda: leaves(par, 6), product[6]] + panel[4:6] + [lambda: leaves(par, 7), product[7]]
+        image = gather_and_multiply(par, tasks, work, panel[6:])
         buf[1 - par, pl.ds(0, BLOCK), :] = exact_dot(image, inverse[...], (((1,), (1,)), ((), ())))
         return carry
 

time: 135 us -> 138 us (1.022)
  Pallas kernels: 134 us -> 136 us
    pallas_call x1, Pallas kernels: 131 us -> 134 us  [per_device(): pl.pallas_call(kernel, out_shape=(narrow, narrow, broad), in_specs=[pl.Bl...]
where the time goes in v7:
time: 138 us
  Pallas kernels  136 us (99%)
    pallas_call x1, Pallas kernels, per_device(): pl.pallas_call(kernel, out_shape=(narrow, narrow, broad), in_specs=[pl.Bl...  134 us

profile of v7, /device:TPU:1, one launch (start us, length us, event | category | flops | bytes accessed | tf_op | source)
XLA Modules:
  0.0 137.6 jit_solution(15190424629908173141)
XLA Ops:
  1.3 134.0 %iterate.1 = (f32[128,128]{1,0:T(8,128)}, f32[128,128]{1,0:T(8,128)}, f32[128,256]{1,0:T(8,128)}) custom-call(f32[128,16384]{1,0:T(8,128)} %kernel_hbm.1, f32[128,128]{1,0:T(8,128)} %start.1, f32[128,256]{1,0:T(8,128)} %test.1, s32[1]{0:T(128)S(6)} %copy.6.cutoff), custom_call_target="tpu_custom_call" | custom-call | flops 8589934592 | bytes 16777216 | tf_op jit(solution)/shard_map/iterate/pallas_call | solution.py:370
  135.3 2.3 %project.1 = (f32[128,128]{1,0:T(8,128)}, f32[128,256]{1,0:T(8,128)}) custom-call(f32[128,128]{1,0:T(8,128)} %get-tuple-element.5.image, f32[128,128]{1,0:T(8,128)} %get-tuple-element.6.inverse, f32[128,256]{1,0:T(8,128)} %get-tuple-element.7.kept), custom_call_target="tpu_custom_call" | custom-call | tf_op jit(solution)/shard_map/project/pallas_call | solution.py:413

commit v8 on v6

--- a/solution.py
+++ b/solution.py
@@ -16,7 +16,8 @@
 TEAM = RING * RING
 LINE = 2 * RING
 PIECE = BLOCK // TEAM
-GROUPED = BLOCK
+WIDTH = 16
+PANELS = BLOCK // WIDTH
 MESH = pl.DeviceIdType.MESH
 HIGHEST = lax.Precision.HIGHEST
 
@@ -56,57 +57,50 @@
     return r * (2.0 - x * r)
 
 
-def eliminate(m, inverse, scale, scaled, panel):
-    base = 8 * panel
-    end = base // GROUPED * GROUPED + GROUPED
+def eliminate(m, inverse, scale, panel):
+    base = WIDTH * panel
+    end = base + WIDTH
     wide = (8, BLOCK)
     lane = lax.broadcasted_iota(jnp.int32, wide, 1)
-    within = (lane >= base) & (lane < base + 8)
-    top = m[base : base + 8, :]
-    raw = [jnp.broadcast_to(top[k : k + 1, :], wide) for k in range(8)]
+    within = (lane >= base) & (lane < end)
+    raw = [jnp.broadcast_to(m[base + k : base + k + 1, :], wide) for k in range(WIDTH)]
     a = {
-        (k, i): jnp.broadcast_to(raw[k][:, base + i : base + i + 1], wide) for k in range(8) for i in range(k, 8)
+        (k, i): jnp.broadcast_to(raw[k][:, base + i : base + i + 1], wide)
+        for k in range(WIDTH)
+        for i in range(k, WIDTH)
     }
-    rows = [jnp.where(within, jnp.where(lane == base + k, 1.0, 0.0), raw[k]) for k in range(8)]
+    rows = [jnp.where(within, jnp.where(lane == base + k, 1.0, 0.0), raw[k]) for k in range(WIDTH)]
     over, factor = {}, {}
-    for k in range(0, 8, 2):
+    for k in range(0, WIDTH, 2):
         p, q, r = a[k, k], a[k, k + 1], a[k + 1, k + 1]
         over[k] = reciprocal(p * r - q * q)
-        for i in range(k + 2, 8):
+        for i in range(k + 2, WIDTH):
             factor[k, i] = (r * a[k, i] - q * a[k + 1, i]) * over[k]
             factor[k + 1, i] = (p * a[k + 1, i] - q * a[k, i]) * over[k]
-            for j in range(i, 8):
+            for j in range(i, WIDTH):
                 a[i, j] = a[i, j] - (factor[k, i] * a[k, j] + factor[k + 1, i] * a[k + 1, j])
             rows[i] = rows[i] - (factor[k, i] * rows[k] + factor[k + 1, i] * rows[k + 1])
-    if base + 8 < end:
-        solved = [None] * 8
-        for k in range(0, 8, 2):
+    if end < BLOCK:
+        solved = [None] * WIDTH
+        for k in range(0, WIDTH, 2):
             p, q, r = a[k, k] * over[k], a[k, k + 1] * over[k], a[k + 1, k + 1] * over[k]
             solved[k] = r * rows[k] - q * rows[k + 1]
             solved[k + 1] = p * rows[k + 1] - q * rows[k]
-        for k in (6, 4, 2):
+        for k in range(WIDTH - 2, 0, -2):
             for i in range(k):
                 solved[i] = solved[i] - (factor[i, k] * solved[k] + factor[i, k + 1] * solved[k + 1])
-        for r in range(base + 8, end, 8):
+        for r in range(end, BLOCK, 8):
             rest = m[r : r + 8, :]
-            terms = [jnp.broadcast_to(rest[:, base + k : base + k + 1], wide) * solved[k] for k in range(8)]
+            terms = [jnp.broadcast_to(rest[:, base + k : base + k + 1], wide) * solved[k] for k in range(WIDTH)]
             while len(terms) > 1:
                 terms = [x + y for x, y in zip(terms[::2], terms[1::2])]
             m[r : r + 8, :] = jnp.where(within, 0.0, rest) - terms[0]
-    for k in range(0, 8, 2):
+    for k in range(0, WIDTH, 2):
         p, q = a[k, k], a[k, k + 1]
-        first = rows[k] * (1.0 / jnp.sqrt(p))
-        second = (rows[k + 1] - rows[k] * (q / p)) * jnp.sqrt(p * over[k])
+        first = rows[k] * (scale[...] / jnp.sqrt(p))
+        second = (rows[k + 1] - rows[k] * (q / p)) * (scale[...] * jnp.sqrt(p * over[k]))
         for j, done in ((base + k, first), (base + k + 1, second)):
-            inverse[j : j + 1, :] = jnp.where(lane < base + 8, done * scale[...], 0.0)[0:1, :]
-            if end < BLOCK:
-                kept = (lane < base + 8) | (lane >= end)
-                scaled[j % GROUPED : j % GROUPED + 1, :] = jnp.where(kept, done, 0.0)[0:1, :]
-    if base + 8 == end and end < BLOCK:
-        done = scaled[...]
-        lanes = lax.broadcasted_iota(jnp.int32, (BLOCK - end, BLOCK), 1)
-        rest = jnp.where((lanes >= end - GROUPED) & (lanes < end), 0.0, m[end:, :])
-        m[end:, :] = rest - exact_dot(done.T[end:, :], done)
+            inverse[j : j + 1, :] = jnp.where(lane < end, done, 0.0)[0:1, :]
 
 
 def load_scaled(value, m, scale):
@@ -120,7 +114,7 @@
 
 def kernel(
     kernel_hbm, start, test, cutoff, image_out, inverse, kept_out,
-    buf, kf, khl, acc, m, scale, scaled, loc, pieces, lines, full, cloc, cpieces, clines, cfull, psend, precv,
+    buf, kf, khl, acc, m, scale, loc, pieces, lines, full, cloc, cpieces, clines, cfull, psend, precv,
     ag_recv, ag_send, k_local, k_recv, k_send, ar_recv, ar_send, cr_recv, cr_send, p_recv, p_send,
 ):
     row, col = lax.axis_index("row"), lax.axis_index("col")
@@ -267,7 +261,7 @@
     def factor_panel(p):
         if p == 0:
             load_scaled(whole_sum(full_now[0]), m, scale)
-        eliminate(m, inverse, scale, scaled, p)
+        eliminate(m, inverse, scale, p)
 
     full_now = [None]
 
@@ -320,13 +314,13 @@
         for at, stage in zip((5, 13), stages[1:3]):
             tasks.setdefault(at, []).append(stage)
         product = [lambda c=c: multiply(par, c) for c in range(SLOTS // CHUNK)]
-        panel = [lambda p=p: factor_panel(p) for p in range(16)]
+        panel = [lambda p=p: factor_panel(p) for p in range(PANELS)]
         for at, c in ((20, 0), (25, 1), (29, 2)):
             tasks.setdefault(at, []).append(product[c])
-        work = [product[3], stages[3]] + panel[0:4]
-        work += [lambda: leaves(par, 4), lambda: leaves(par, 5), product[4], product[5]] + panel[4:8]
-        work += [lambda: leaves(par, 6), product[6]] + panel[8:12] + [lambda: leaves(par, 7), product[7]]
-        image = gather_and_multiply(par, tasks, work, panel[12:])
+        work = [product[3], stages[3]] + panel[0:2]
+        work += [lambda: leaves(par, 4), lambda: leaves(par, 5), product[4], product[5]] + panel[2:4]
+        work += [lambda: leaves(par, 6), product[6]] + panel[4:6] + [lambda: leaves(par, 7), product[7]]
+        image = gather_and_multiply(par, tasks, work, panel[6:])
         buf[1 - par, pl.ds(0, BLOCK), :] = exact_dot(image, inverse[...], (((1,), (1,)), ((), ())))
         return carry
 
@@ -346,8 +340,8 @@
     stages[2]()
     late[2]()
     stages[3]()
-    for p in range(16):
-        if p == 8:
+    for p in range(PANELS):
+        if p == PANELS // 2:
             late[3]()
         factor_panel(p)
     image_out[...] = buf[par, pl.ds(0, BLOCK), :]
@@ -380,7 +374,6 @@
             pltpu.VMEM((4 * BLOCK, 2 * BLOCK), f32),
             pltpu.VMEM((BLOCK, BLOCK), f32),
             pltpu.VMEM((8, BLOCK), f32),
-            pltpu.VMEM((GROUPED, BLOCK), f32),
             pltpu.VMEM((BLOCK, BLOCK), f32),
             pltpu.VMEM((2, TEAM, PIECE, BLOCK), f32),
             pltpu.VMEM((2, LINE, PIECE, BLOCK), f32),

time: 135 us -> 138 us (1.022)
  Pallas kernels: 134 us -> 137 us
    pallas_call x1, Pallas kernels: 131 us -> 135 us  [per_device(): pl.pallas_call(kernel, out_shape=(narrow, narrow, broad), in_specs=[pl.Bl...]
where the time goes in v8:
time: 138 us
  Pallas kernels  137 us (99%)
    pallas_call x1, Pallas kernels, per_device(): pl.pallas_call(kernel, out_shape=(narrow, narrow, broad), in_specs=[pl.Bl...  135 us

profile of v8, /device:TPU:1, one launch (start us, length us, event | category | flops | bytes accessed | tf_op | source)
XLA Modules:
  0.0 138.3 jit_solution(15654428020425491527)
XLA Ops:
  1.3 134.8 %iterate.1 = (f32[128,128]{1,0:T(8,128)}, f32[128,128]{1,0:T(8,128)}, f32[128,256]{1,0:T(8,128)}) custom-call(f32[128,16384]{1,0:T(8,128)} %kernel_hbm.1, f32[128,128]{1,0:T(8,128)} %start.1, f32[128,256]{1,0:T(8,128)} %test.1, s32[1]{0:T(128)S(6)} %copy.6.cutoff), custom_call_target="tpu_custom_call" | custom-call | flops 8589934592 | bytes 16777216 | tf_op jit(solution)/shard_map/iterate/pallas_call | solution.py:365
  136.0 2.3 %project.1 = (f32[128,128]{1,0:T(8,128)}, f32[128,256]{1,0:T(8,128)}) custom-call(f32[128,128]{1,0:T(8,128)} %get-tuple-element.5.image, f32[128,128]{1,0:T(8,128)} %get-tuple-element.6.inverse, f32[128,256]{1,0:T(8,128)} %get-tuple-element.7.kept), custom_call_target="tpu_custom_call" | custom-call | tf_op jit(solution)/shard_map/project/pallas_call | solution.py:407

commit v9 on v6

--- a/solution.py
+++ b/solution.py
@@ -21,28 +21,32 @@
 HIGHEST = lax.Precision.HIGHEST
 
 TREE = (
-    0, 768, 3072, 64, 448, 256, 1088, 1024, 3840, 832, 320, 961, 708, 2050, 3138, 4033,
-    1732, 3333, 131, 1223, 3592, 1287, 3913, 1354, 2182, 585, 2317, 1995, 1158, 652, 2768, 3218,
-    192, 3264, 513, 1793, 1862, 907, 2126, 2829, 394, 1491, 3791, 3983, 2259, 3409, 2580, 1557,
-    3670, 3537, 1431, 1625, 2902, 2456, 2968, 2522, 3035, 2394, 3741, 1948, 2718, 1693, 2650, 3487,
+    0, 49152, 196608, 65536, 28672, 16384, 12288, 69632, 4096, 114753, 131202, 53313,
+    61506, 32836, 78019, 110852, 213317, 201224, 148106, 24840, 139719, 258828, 37579, 58059,
+    127756, 250575, 119245, 45901, 177104, 208896, 20480, 245890, 82119, 98889, 8713, 74121,
+    180878, 95118, 107472, 205905, 86479, 160914, 136273, 218193, 144276, 152722, 243029, 189717,
+    103831, 169108, 222419, 230227, 226330, 194072, 255447, 91355, 124570, 42715, 165018, 156954,
+    235100, 173852, 239193, 185948,
 )
-ORDER = [(code // 1024, code // 256 % 4, code // 64 % 4) for code in TREE]
-PARENT = [code % 64 for code in TREE]
+ORDER = [(code // 65536, code // 16384 % 4, code // 4096 % 4) for code in TREE]
+PARENT = [code // 64 % 64 for code in TREE]
+AFTER = [code % 64 for code in TREE]
 
 
 def passed_on():
-    children = [[] for _ in TREE]
     height = [0] * SLOTS
     for s in reversed(range(1, SLOTS)):
-        children[PARENT[s]].append(s)
         height[PARENT[s]] = max(height[PARENT[s]], height[s] + 1)
-    for found in children:
-        found.sort(key=lambda s: -height[s])
-    return children
-
-
-CHILDREN = passed_on()
-INNER = sum(1 for found in CHILDREN if found)
+    sent = [[] for _ in TREE]
+    for s in range(1, SLOTS):
+        sent[AFTER[s]].append(s)
+    for at, found in enumerate(sent):
+        found.sort(key=lambda s: (PARENT[s] != at, -height[s]))
+    return sent
+
+
+SENT = passed_on()
+INNER = len(set(PARENT))
 GROUP = [s if s < INNER else max(INNER, s // CHUNK * CHUNK) for s in range(SLOTS)]
 
 
@@ -54,6 +58,11 @@
     r = pl.reciprocal(x, approx=True)
     r = r * (2.0 - x * r)
     return r * (2.0 - x * r)
+
+
+def inverse_root(x):
+    r = lax.rsqrt(x)
+    return r * (1.5 - 0.5 * x * r * r)
 
 
 def eliminate(m, inverse, scale, scaled, panel):
@@ -95,8 +104,10 @@
             m[r : r + 8, :] = jnp.where(within, 0.0, rest) - terms[0]
     for k in range(0, 8, 2):
         p, q = a[k, k], a[k, k + 1]
-        first = rows[k] * (1.0 / jnp.sqrt(p))
-        second = (rows[k + 1] - rows[k] * (q / p)) * jnp.sqrt(p * over[k])
+        r = inverse_root(p)
+        ratio = p * over[k]
+        first = rows[k] * r
+        second = (rows[k + 1] - rows[k] * (q * r * r)) * (ratio * inverse_root(ratio))
         for j, done in ((base + k, first), (base + k + 1, second)):
             inverse[j : j + 1, :] = jnp.where(lane < base + 8, done * scale[...], 0.0)[0:1, :]
             if end < BLOCK:
@@ -161,9 +172,9 @@
         return buf.at[par, pl.ds(s * BLOCK, count * BLOCK)]
 
     def forward(par, s):
-        for child in CHILDREN[s]:
+        for child in SENT[s]:
             remote(
-                block(par, s), block(par, child), ag_send, ag_recv.at[par, GROUP[child]], moved(hop(child))
+                block(par, PARENT[child]), block(par, child), ag_send, ag_recv.at[par, GROUP[child]], moved(hop(child))
             ).start()
 
     def arrived(par, group):
@@ -304,7 +315,7 @@
         tasks.setdefault((s * 2) // 5, []).append(lambda s=s: start_kernel_copies(s))
     work = []
     for c in range(SLOTS // CHUNK):
-        into = tasks.setdefault((25, 29)[c], []) if c < 2 else work
+        into = tasks.setdefault((17, 23)[c], []) if c < 2 else work
         into += [lambda c=c: split_kernel(c), lambda c=c: leaves(0, c), lambda c=c: multiply(0, c)]
     image = gather_and_multiply(0, tasks, work, [])
     buf[1, pl.ds(0, BLOCK), :] = image
@@ -317,15 +328,15 @@
         stages = sum_stages(loc, pieces.at[par], lines.at[par], full.at[par], ar_recv.at[par], ar_send)
         full_now[0] = full.at[par]
         tasks = {0: [lambda: local_gram(par), stages[0]]}
-        for at, stage in zip((5, 13), stages[1:3]):
+        for at, stage in zip((3, 12), stages[1:3]):
             tasks.setdefault(at, []).append(stage)
         product = [lambda c=c: multiply(par, c) for c in range(SLOTS // CHUNK)]
         panel = [lambda p=p: factor_panel(p) for p in range(16)]
-        for at, c in ((20, 0), (25, 1), (29, 2)):
+        for at, c in ((13, 0), (17, 1), (23, 2)):
             tasks.setdefault(at, []).append(product[c])
-        work = [product[3], stages[3]] + panel[0:4]
-        work += [lambda: leaves(par, 4), lambda: leaves(par, 5), product[4], product[5]] + panel[4:8]
-        work += [lambda: leaves(par, 6), product[6]] + panel[8:12] + [lambda: leaves(par, 7), product[7]]
+        work = [stages[3]] + panel[0:4] + [lambda: leaves(par, 3), product[3]] + panel[4:8]
+        work += [lambda: leaves(par, 4), product[4]] + panel[8:12] + [lambda: leaves(par, 5), product[5]]
+        work += [lambda: leaves(par, 6), product[6], lambda: leaves(par, 7), product[7]]
         image = gather_and_multiply(par, tasks, work, panel[12:])
         buf[1 - par, pl.ds(0, BLOCK), :] = exact_dot(image, inverse[...], (((1,), (1,)), ((), ())))
         return carry

time: 135 us -> 133 us (0.985)
  Pallas kernels: 134 us -> 132 us
    pallas_call x1, Pallas kernels: 131 us -> 130 us  [per_device(): pl.pallas_call(kernel, out_shape=(narrow, narrow, broad), in_specs=[pl.Bl...]
where the time goes in v9:
time: 133 us
  Pallas kernels  132 us (99%)
    pallas_call x1, Pallas kernels, per_device(): pl.pallas_call(kernel, out_shape=(narrow, narrow, broad), in_specs=[pl.Bl...  130 us

profile of v9, /device:TPU:1, one launch (start us, length us, event | category | flops | bytes accessed | tf_op | source)
XLA Modules:
  0.0 133.2 jit_solution(15947361530459008587)
XLA Ops:
  1.3 129.7 %iterate.1 = (f32[128,128]{1,0:T(8,128)}, f32[128,128]{1,0:T(8,128)}, f32[128,256]{1,0:T(8,128)}) custom-call(f32[128,16384]{1,0:T(8,128)} %kernel_hbm.1, f32[128,128]{1,0:T(8,128)} %start.1, f32[128,256]{1,0:T(8,128)} %test.1, s32[1]{0:T(128)S(6)} %copy.6.cutoff), custom_call_target="tpu_custom_call" | custom-call | flops 8589934592 | bytes 16777216 | tf_op jit(solution)/shard_map/iterate/pallas_call | solution.py:382
  131.0 2.3 %project.1 = (f32[128,128]{1,0:T(8,128)}, f32[128,256]{1,0:T(8,128)}) custom-call(f32[128,128]{1,0:T(8,128)} %get-tuple-element.5.image, f32[128,128]{1,0:T(8,128)} %get-tuple-element.6.inverse, f32[128,256]{1,0:T(8,128)} %get-tuple-element.7.kept), custom_call_target="tpu_custom_call" | custom-call | tf_op jit(solution)/shard_map/project/pallas_call | solution.py:425

commit v10 on v9

--- a/solution.py
+++ b/solution.py
@@ -13,6 +13,7 @@
 RING = 4
 SLOTS = RING**3
 CHUNK = 8
+PARTS = 4
 TEAM = RING * RING
 LINE = 2 * RING
 PIECE = BLOCK // TEAM
@@ -131,7 +132,7 @@
 
 def kernel(
     kernel_hbm, start, test, cutoff, image_out, inverse, kept_out,
-    buf, kf, khl, acc, m, scale, scaled, loc, pieces, lines, full, cloc, cpieces, clines, cfull, psend, precv,
+    buf, kall, kgive, kget, khl, acc, m, scale, scaled, loc, pieces, lines, full, cloc, cpieces, clines, cfull, psend, precv,
     ag_recv, ag_send, k_local, k_recv, k_send, ar_recv, ar_send, cr_recv, cr_send, p_recv, p_send,
 ):
     row, col = lax.axis_index("row"), lax.axis_index("col")
@@ -158,6 +159,7 @@
     greet = [moved(by) for by in sorted(near - {(0, 0, 0)})]
     greet += [moved((0, 0, z), 1 - core) for z in range(RING)]
 
+    pltpu.make_async_copy(kernel_hbm, kall, k_local).start()
     barrier = pltpu.get_barrier_semaphore()
     for other in greet:
         pl.semaphore_signal(barrier, inc=1, device_id=other, device_id_type=MESH)
@@ -181,32 +183,40 @@
         whole = block(par, group, GROUP.count(group))
         pltpu.make_async_copy(whole, whole, ag_recv.at[par, group]).wait()
 
-    def columns(s, c):
+    def rank(s):
         x, y, z = [lax.rem(p + RING - d, RING) for p, d in zip(here, ORDER[s])]
-        r, q = device(x, y, z, c)
-        return pl.ds(pl.multiple_of((r * 16 + q) * BLOCK, BLOCK), BLOCK)
+        return (z * 2 + lax.rem(x, 2)) * 8 + y * 2 + lax.div(x, 2)
+
+    def columns(j):
+        return pl.ds(pl.multiple_of(j * BLOCK, BLOCK), BLOCK)
 
     def lanes(c):
         return pl.ds(c * CHUNK * BLOCK, CHUNK * BLOCK)
 
-    def start_kernel_copies(s):
-        c, there = s // CHUNK, pl.ds(s * BLOCK, BLOCK)
-        remote(
-            kernel_hbm.at[:, columns(s, 1 - core)], kf.at[pl.ds(BLOCK, BLOCK), there],
-            k_send.at[c], k_recv.at[c], sibling,
-        ).start()
-        pltpu.make_async_copy(
-            kernel_hbm.at[:, columns(s, core)], kf.at[pl.ds(0, BLOCK), there], k_local.at[c]
-        ).start()
-
-    def split_kernel(c):
-        own, other = kf.at[pl.ds(0, BLOCK), lanes(c)], kf.at[pl.ds(BLOCK, BLOCK), lanes(c)]
-        pltpu.make_async_copy(own, own, k_local.at[c]).wait()
-        pltpu.make_async_copy(other, other, k_recv.at[c]).wait()
-        value = kf[:, lanes(c)]
-        high = value.astype(jnp.bfloat16)
-        khl[0 : 2 * BLOCK, lanes(c)] = high
-        khl[2 * BLOCK : 4 * BLOCK, lanes(c)] = (value - high.astype(jnp.float32)).astype(jnp.bfloat16)
+    def part_of_given(c):
+        return pl.ds(c * (SLOTS // PARTS) * BLOCK, (SLOTS // PARTS) * BLOCK)
+
+    def give_kernel():
+        pltpu.make_async_copy(kernel_hbm, kall, k_local).wait()
+        for c in range(PARTS):
+            for j in range(c * (SLOTS // PARTS), (c + 1) * (SLOTS // PARTS)):
+                kgive[:, j * BLOCK : (j + 1) * BLOCK] = kall[:, columns(2 * j + 1 - core)]
+            there = part_of_given(c)
+            remote(kgive.at[:, there], kget.at[:, there], k_send.at[c], k_recv.at[c], sibling).start()
+
+    def given_kernel(c):
+        there = part_of_given(c)
+        remote(kgive.at[:, there], kget.at[:, there], k_send.at[c], k_recv.at[c], sibling).wait()
+
+    def split_kernel(c, own):
+        for s in range(c * CHUNK, (c + 1) * CHUNK):
+            j = rank(s)
+            value = kall[:, columns(2 * j + core)] if own else kget[:, columns(j)]
+            high = value.astype(jnp.bfloat16)
+            low = (value - high.astype(jnp.float32)).astype(jnp.bfloat16)
+            first, there = 0 if own else BLOCK, slice(s * BLOCK, (s + 1) * BLOCK)
+            khl[first : first + BLOCK, there] = high
+            khl[2 * BLOCK + first : 3 * BLOCK + first, there] = low
 
     def leaves(par, c):
         for group in sorted(set(GROUP[c * CHUNK : (c + 1) * CHUNK])):
@@ -310,18 +320,13 @@
         loc[...] = exact_dot(y.T, y)
 
     buf[0, pl.ds(0, BLOCK), :] = start[...]
-    tasks = {}
-    for s in range(SLOTS):
-        tasks.setdefault((s * 2) // 5, []).append(lambda s=s: start_kernel_copies(s))
-    work = []
+    tasks = {0: [give_kernel]}
+    work = [lambda c=c: given_kernel(c) for c in range(PARTS)]
     for c in range(SLOTS // CHUNK):
-        into = tasks.setdefault((17, 23)[c], []) if c < 2 else work
-        into += [lambda c=c: split_kernel(c), lambda c=c: leaves(0, c), lambda c=c: multiply(0, c)]
+        tasks[10 + 2 * c] = [lambda c=c: split_kernel(c, True)]
+        work += [lambda c=c: split_kernel(c, False), lambda c=c: leaves(0, c), lambda c=c: multiply(0, c)]
     image = gather_and_multiply(0, tasks, work, [])
     buf[1, pl.ds(0, BLOCK), :] = image
-    for c in range(SLOTS // CHUNK):
-        given = kf.at[pl.ds(0, BLOCK), lanes(c)]
-        pltpu.make_async_copy(given, given, k_send.at[c]).wait()
 
     def step(t, carry):
         par = lax.rem(t, 2)
@@ -376,7 +381,6 @@
     f32 = jnp.float32
     vmem = pl.BlockSpec(memory_space=pltpu.VMEM)
     dma = pltpu.SemaphoreType.DMA
-    chunks = SLOTS // CHUNK
     narrow = jax.ShapeDtypeStruct((BLOCK, BLOCK), f32)
     broad = jax.ShapeDtypeStruct((BLOCK, TEST), f32)
     image, inverse, kept = pl.pallas_call(
@@ -386,7 +390,9 @@
         out_specs=(vmem, vmem, vmem),
         scratch_shapes=[
             pltpu.VMEM((2, SLOTS * BLOCK, BLOCK), f32),
-            pltpu.VMEM((2 * BLOCK, SLOTS * BLOCK), f32),
+            pltpu.VMEM((BLOCK, 2 * SLOTS * BLOCK), f32),
+            pltpu.VMEM((BLOCK, SLOTS * BLOCK), f32),
+            pltpu.VMEM((BLOCK, SLOTS * BLOCK), f32),
             pltpu.VMEM((4 * BLOCK, SLOTS * BLOCK), jnp.bfloat16),
             pltpu.VMEM((4 * BLOCK, 2 * BLOCK), f32),
             pltpu.VMEM((BLOCK, BLOCK), f32),
@@ -404,9 +410,9 @@
             pltpu.VMEM((2, BLOCK, BLOCK), f32),
             dma((2, SLOTS)),
             dma,
-            dma((chunks,)),
-            dma((chunks,)),
-            dma((chunks,)),
+            dma,
+            dma((PARTS,)),
+            dma((PARTS,)),
             dma((2, 3)),
             dma((3,)),
             dma((3,)),

time: 133 us -> 133 us (level)
  no operation moved by 1% of the time
where the time goes in v10:
time: 133 us
  Pallas kernels  132 us (99%)
    pallas_call x1, Pallas kernels, per_device(): pl.pallas_call(kernel, out_shape=(narrow, narrow, broad), in_specs=[pl.Bl...  129 us

profile of v10, /device:TPU:1, one launch (start us, length us, event | category | flops | bytes accessed | tf_op | source)
XLA Modules:
  0.0 132.8 jit_solution(13037930668697268478)
XLA Ops:
  1.3 129.3 %iterate.1 = (f32[128,128]{1,0:T(8,128)}, f32[128,128]{1,0:T(8,128)}, f32[128,256]{1,0:T(8,128)}) custom-call(f32[128,16384]{1,0:T(8,128)} %kernel_hbm.1, f32[128,128]{1,0:T(8,128)} %start.1, f32[128,256]{1,0:T(8,128)} %test.1, s32[1]{0:T(128)S(6)} %copy.6.cutoff), custom_call_target="tpu_custom_call" | custom-call | flops 8589934592 | bytes 16777216 | tf_op jit(solution)/shard_map/iterate/pallas_call | solution.py:386
  130.5 2.3 %project.1 = (f32[128,128]{1,0:T(8,128)}, f32[128,256]{1,0:T(8,128)}) custom-call(f32[128,128]{1,0:T(8,128)} %get-tuple-element.5.image, f32[128,128]{1,0:T(8,128)} %get-tuple-element.6.inverse, f32[128,256]{1,0:T(8,128)} %get-tuple-element.7.kept), custom_call_target="tpu_custom_call" | custom-call | tf_op jit(solution)/shard_map/project/pallas_call | solution.py:431

commit v11 on v10

--- a/solution.py
+++ b/solution.py
@@ -333,14 +333,14 @@
         stages = sum_stages(loc, pieces.at[par], lines.at[par], full.at[par], ar_recv.at[par], ar_send)
         full_now[0] = full.at[par]
         tasks = {0: [lambda: local_gram(par), stages[0]]}
-        for at, stage in zip((3, 12), stages[1:3]):
+        for at, stage in zip((0, 8, 24), stages[1:]):
             tasks.setdefault(at, []).append(stage)
         product = [lambda c=c: multiply(par, c) for c in range(SLOTS // CHUNK)]
         panel = [lambda p=p: factor_panel(p) for p in range(16)]
-        for at, c in ((13, 0), (17, 1), (23, 2)):
-            tasks.setdefault(at, []).append(product[c])
-        work = [stages[3]] + panel[0:4] + [lambda: leaves(par, 3), product[3]] + panel[4:8]
-        work += [lambda: leaves(par, 4), product[4]] + panel[8:12] + [lambda: leaves(par, 5), product[5]]
+        for at, task in [(13, product[0]), (17, product[1])] + [(25 + p // 2, panel[p]) for p in range(8)]:
+            tasks.setdefault(at, []).append(task)
+        work = [product[2], lambda: leaves(par, 3), product[3]] + panel[8:10]
+        work += [lambda: leaves(par, 4), product[4]] + panel[10:12] + [lambda: leaves(par, 5), product[5]]
         work += [lambda: leaves(par, 6), product[6], lambda: leaves(par, 7), product[7]]
         image = gather_and_multiply(par, tasks, work, panel[12:])
         buf[1 - par, pl.ds(0, BLOCK), :] = exact_dot(image, inverse[...], (((1,), (1,)), ((), ())))

time: 133 us -> 139 us (1.045)
  Pallas kernels: 132 us -> 137 us
    pallas_call x1, Pallas kernels: 129 us -> 135 us  [per_device(): pl.pallas_call(kernel, out_shape=(narrow, narrow, broad), in_specs=[pl.Bl...]
where the time goes in v11:
time: 139 us; the launch traced here: 138 us
  Pallas kernels  137 us (99%)
    pallas_call x1, Pallas kernels, per_device(): pl.pallas_call(kernel, out_shape=(narrow, narrow, broad), in_specs=[pl.Bl...  135 us

profile of v11, /device:TPU:1, one launch (start us, length us, event | category | flops | bytes accessed | tf_op | source)
XLA Modules:
  0.0 138.5 jit_solution(4783384522927684818)
XLA Ops:
  1.3 134.9 %iterate.1 = (f32[128,128]{1,0:T(8,128)}, f32[128,128]{1,0:T(8,128)}, f32[128,256]{1,0:T(8,128)}) custom-call(f32[128,16384]{1,0:T(8,128)} %kernel_hbm.1, f32[128,128]{1,0:T(8,128)} %start.1, f32[128,256]{1,0:T(8,128)} %test.1, s32[1]{0:T(128)S(6)} %copy.6.cutoff), custom_call_target="tpu_custom_call" | custom-call | flops 8589934592 | bytes 16777216 | tf_op jit(solution)/shard_map/iterate/pallas_call | solution.py:386
  136.2 2.3 %project.1 = (f32[128,128]{1,0:T(8,128)}, f32[128,256]{1,0:T(8,128)}) custom-call(f32[128,128]{1,0:T(8,128)} %get-tuple-element.5.image, f32[128,128]{1,0:T(8,128)} %get-tuple-element.6.inverse, f32[128,256]{1,0:T(8,128)} %get-tuple-element.7.kept), custom_call_target="tpu_custom_call" | custom-call | tf_op jit(solution)/shard_map/project/pallas_call | solution.py:431

commit v12 on v10

--- a/solution.py
+++ b/solution.py
@@ -333,16 +333,16 @@
         stages = sum_stages(loc, pieces.at[par], lines.at[par], full.at[par], ar_recv.at[par], ar_send)
         full_now[0] = full.at[par]
         tasks = {0: [lambda: local_gram(par), stages[0]]}
-        for at, stage in zip((3, 12), stages[1:3]):
+        for at, stage in zip((6, 18), stages[1:3]):
             tasks.setdefault(at, []).append(stage)
         product = [lambda c=c: multiply(par, c) for c in range(SLOTS // CHUNK)]
         panel = [lambda p=p: factor_panel(p) for p in range(16)]
-        for at, c in ((13, 0), (17, 1), (23, 2)):
+        for at, c in ((13, 0), (17, 1)):
             tasks.setdefault(at, []).append(product[c])
-        work = [stages[3]] + panel[0:4] + [lambda: leaves(par, 3), product[3]] + panel[4:8]
-        work += [lambda: leaves(par, 4), product[4]] + panel[8:12] + [lambda: leaves(par, 5), product[5]]
+        work = [product[2], lambda: leaves(par, 3), product[3], lambda: leaves(par, 4), product[4], stages[3]]
+        work += panel[0:6] + [lambda: leaves(par, 5), product[5]] + panel[6:10]
         work += [lambda: leaves(par, 6), product[6], lambda: leaves(par, 7), product[7]]
-        image = gather_and_multiply(par, tasks, work, panel[12:])
+        image = gather_and_multiply(par, tasks, work, panel[10:])
         buf[1 - par, pl.ds(0, BLOCK), :] = exact_dot(image, inverse[...], (((1,), (1,)), ((), ())))
         return carry
 

time: 133 us -> 131 us (0.985)
  Pallas kernels: 132 us -> 129 us
    pallas_call x1, Pallas kernels: 129 us -> 127 us  [per_device(): pl.pallas_call(kernel, out_shape=(narrow, narrow, broad), in_specs=[pl.Bl...]
where the time goes in v12:
time: 131 us; the launch traced here: 130 us
  Pallas kernels  129 us (98%)
    pallas_call x1, Pallas kernels, per_device(): pl.pallas_call(kernel, out_shape=(narrow, narrow, broad), in_specs=[pl.Bl...  127 us

profile of v12, /device:TPU:1, one launch (start us, length us, event | category | flops | bytes accessed | tf_op | source)
XLA Modules:
  0.0 130.4 jit_solution(8247413082863781375)
XLA Ops:
  1.3 126.8 %iterate.1 = (f32[128,128]{1,0:T(8,128)}, f32[128,128]{1,0:T(8,128)}, f32[128,256]{1,0:T(8,128)}) custom-call(f32[128,16384]{1,0:T(8,128)} %kernel_hbm.1, f32[128,128]{1,0:T(8,128)} %start.1, f32[128,256]{1,0:T(8,128)} %test.1, s32[1]{0:T(128)S(6)} %copy.6.cutoff), custom_call_target="tpu_custom_call" | custom-call | flops 8589934592 | bytes 16777216 | tf_op jit(solution)/shard_map/iterate/pallas_call | solution.py:386
  128.1 2.3 %project.1 = (f32[128,128]{1,0:T(8,128)}, f32[128,256]{1,0:T(8,128)}) custom-call(f32[128,128]{1,0:T(8,128)} %get-tuple-element.5.image, f32[128,128]{1,0:T(8,128)} %get-tuple-element.6.inverse, f32[128,256]{1,0:T(8,128)} %get-tuple-element.7.kept), custom_call_target="tpu_custom_call" | custom-call | tf_op jit(solution)/shard_map/project/pallas_call | solution.py:431

commit v13 on v12

--- a/solution.py
+++ b/solution.py
@@ -333,13 +333,11 @@
         stages = sum_stages(loc, pieces.at[par], lines.at[par], full.at[par], ar_recv.at[par], ar_send)
         full_now[0] = full.at[par]
         tasks = {0: [lambda: local_gram(par), stages[0]]}
-        for at, stage in zip((6, 18), stages[1:3]):
+        for at, stage in zip((9, 22), stages[1:3]):
             tasks.setdefault(at, []).append(stage)
         product = [lambda c=c: multiply(par, c) for c in range(SLOTS // CHUNK)]
         panel = [lambda p=p: factor_panel(p) for p in range(16)]
-        for at, c in ((13, 0), (17, 1)):
-            tasks.setdefault(at, []).append(product[c])
-        work = [product[2], lambda: leaves(par, 3), product[3], lambda: leaves(par, 4), product[4], stages[3]]
+        work = product[0:3] + [lambda: leaves(par, 3), product[3], lambda: leaves(par, 4), product[4], stages[3]]
         work += panel[0:6] + [lambda: leaves(par, 5), product[5]] + panel[6:10]
         work += [lambda: leaves(par, 6), product[6], lambda: leaves(par, 7), product[7]]
         image = gather_and_multiply(par, tasks, work, panel[10:])

time: 131 us -> 136 us (1.038)
  Pallas kernels: 129 us -> 135 us
    pallas_call x1, Pallas kernels: 127 us -> 132 us  [per_device(): pl.pallas_call(kernel, out_shape=(narrow, narrow, broad), in_specs=[pl.Bl...]
where the time goes in v13:
time: 136 us
  Pallas kernels  135 us (99%)
    pallas_call x1, Pallas kernels, per_device(): pl.pallas_call(kernel, out_shape=(narrow, narrow, broad), in_specs=[pl.Bl...  132 us

profile of v13, /device:TPU:1, one launch (start us, length us, event | category | flops | bytes accessed | tf_op | source)
XLA Modules:
  0.0 135.9 jit_solution(135956481870908180)
XLA Ops:
  1.3 132.3 %iterate.1 = (f32[128,128]{1,0:T(8,128)}, f32[128,128]{1,0:T(8,128)}, f32[128,256]{1,0:T(8,128)}) custom-call(f32[128,16384]{1,0:T(8,128)} %kernel_hbm.1, f32[128,128]{1,0:T(8,128)} %start.1, f32[128,256]{1,0:T(8,128)} %test.1, s32[1]{0:T(128)S(6)} %copy.6.cutoff), custom_call_target="tpu_custom_call" | custom-call | flops 8589934592 | bytes 16777216 | tf_op jit(solution)/shard_map/iterate/pallas_call | solution.py:384
  133.6 2.3 %project.1 = (f32[128,128]{1,0:T(8,128)}, f32[128,256]{1,0:T(8,128)}) custom-call(f32[128,128]{1,0:T(8,128)} %get-tuple-element.5.image, f32[128,128]{1,0:T(8,128)} %get-tuple-element.6.inverse, f32[128,256]{1,0:T(8,128)} %get-tuple-element.7.kept), custom_call_target="tpu_custom_call" | custom-call | tf_op jit(solution)/shard_map/project/pallas_call | solution.py:429

commit v14 on v13

--- a/solution.py
+++ b/solution.py
@@ -333,11 +333,13 @@
         stages = sum_stages(loc, pieces.at[par], lines.at[par], full.at[par], ar_recv.at[par], ar_send)
         full_now[0] = full.at[par]
         tasks = {0: [lambda: local_gram(par), stages[0]]}
-        for at, stage in zip((9, 22), stages[1:3]):
+        for at, stage in zip((5, 16), stages[1:3]):
             tasks.setdefault(at, []).append(stage)
         product = [lambda c=c: multiply(par, c) for c in range(SLOTS // CHUNK)]
         panel = [lambda p=p: factor_panel(p) for p in range(16)]
-        work = product[0:3] + [lambda: leaves(par, 3), product[3], lambda: leaves(par, 4), product[4], stages[3]]
+        for at, c in ((11, 0), (17, 1), (23, 2)):
+            tasks.setdefault(at, []).append(product[c])
+        work = [lambda: leaves(par, 3), product[3], lambda: leaves(par, 4), product[4], stages[3]]
         work += panel[0:6] + [lambda: leaves(par, 5), product[5]] + panel[6:10]
         work += [lambda: leaves(par, 6), product[6], lambda: leaves(par, 7), product[7]]
         image = gather_and_multiply(par, tasks, work, panel[10:])

time: 136 us -> 131 us (0.963)
  Pallas kernels: 135 us -> 129 us
    pallas_call x1, Pallas kernels: 132 us -> 127 us  [per_device(): pl.pallas_call(kernel, out_shape=(narrow, narrow, broad), in_specs=[pl.Bl...]
where the time goes in v14:
time: 131 us
  Pallas kernels  129 us (98%)
    pallas_call x1, Pallas kernels, per_device(): pl.pallas_call(kernel, out_shape=(narrow, narrow, broad), in_specs=[pl.Bl...  127 us

profile of v14, /device:TPU:1, one launch (start us, length us, event | category | flops | bytes accessed | tf_op | source)
XLA Modules:
  0.0 130.5 jit_solution(7490841933928765695)
XLA Ops:
  1.3 127.0 %iterate.1 = (f32[128,128]{1,0:T(8,128)}, f32[128,128]{1,0:T(8,128)}, f32[128,256]{1,0:T(8,128)}) custom-call(f32[128,16384]{1,0:T(8,128)} %kernel_hbm.1, f32[128,128]{1,0:T(8,128)} %start.1, f32[128,256]{1,0:T(8,128)} %test.1, s32[1]{0:T(128)S(6)} %copy.6.cutoff), custom_call_target="tpu_custom_call" | custom-call | flops 8589934592 | bytes 16777216 | tf_op jit(solution)/shard_map/iterate/pallas_call | solution.py:386
  128.3 2.3 %project.1 = (f32[128,128]{1,0:T(8,128)}, f32[128,256]{1,0:T(8,128)}) custom-call(f32[128,128]{1,0:T(8,128)} %get-tuple-element.5.image, f32[128,128]{1,0:T(8,128)} %get-tuple-element.6.inverse, f32[128,256]{1,0:T(8,128)} %get-tuple-element.7.kept), custom_call_target="tpu_custom_call" | custom-call | tf_op jit(solution)/shard_map/project/pallas_call | solution.py:431

commit v15 on v12

--- a/solution.py
+++ b/solution.py
@@ -358,12 +358,13 @@
     cloc[...] = exact_dot(last.T, test[...])
     late[0]()
     stages[1]()
+    stages[2]()
     late[1]()
-    stages[2]()
-    late[2]()
     stages[3]()
     for p in range(16):
-        if p == 8:
+        if p == 4:
+            late[2]()
+        if p == 12:
             late[3]()
         factor_panel(p)
     image_out[...] = buf[par, pl.ds(0, BLOCK), :]

time: 131 us -> 133 us (1.015)
  Pallas kernels: 129 us -> 131 us
    pallas_call x1, Pallas kernels: 127 us -> 129 us  [per_device(): pl.pallas_call(kernel, out_shape=(narrow, narrow, broad), in_specs=[pl.Bl...]
where the time goes in v15:
time: 133 us
  Pallas kernels  131 us (98%)
    pallas_call x1, Pallas kernels, per_device(): pl.pallas_call(kernel, out_shape=(narrow, narrow, broad), in_specs=[pl.Bl...  129 us

profile of v15, /device:TPU:1, one launch (start us, length us, event | category | flops | bytes accessed | tf_op | source)
XLA Modules:
  0.0 132.6 jit_solution(7085605226676031423)
XLA Ops:
  1.3 129.1 %iterate.1 = (f32[128,128]{1,0:T(8,128)}, f32[128,128]{1,0:T(8,128)}, f32[128,256]{1,0:T(8,128)}) custom-call(f32[128,16384]{1,0:T(8,128)} %kernel_hbm.1, f32[128,128]{1,0:T(8,128)} %start.1, f32[128,256]{1,0:T(8,128)} %test.1, s32[1]{0:T(128)S(6)} %copy.6.cutoff), custom_call_target="tpu_custom_call" | custom-call | flops 8589934592 | bytes 16777216 | tf_op jit(solution)/shard_map/iterate/pallas_call | solution.py:387
  130.4 2.3 %project.1 = (f32[128,128]{1,0:T(8,128)}, f32[128,256]{1,0:T(8,128)}) custom-call(f32[128,128]{1,0:T(8,128)} %get-tuple-element.5.image, f32[128,128]{1,0:T(8,128)} %get-tuple-element.6.inverse, f32[128,256]{1,0:T(8,128)} %get-tuple-element.7.kept), custom_call_target="tpu_custom_call" | custom-call | tf_op jit(solution)/shard_map/project/pallas_call | solution.py:432

commit v16 on v12

--- a/solution.py
+++ b/solution.py
@@ -340,9 +340,9 @@
         for at, c in ((13, 0), (17, 1)):
             tasks.setdefault(at, []).append(product[c])
         work = [product[2], lambda: leaves(par, 3), product[3], lambda: leaves(par, 4), product[4], stages[3]]
-        work += panel[0:6] + [lambda: leaves(par, 5), product[5]] + panel[6:10]
+        work += panel[0:6] + [lambda: leaves(par, 5), product[5]] + panel[6:8]
         work += [lambda: leaves(par, 6), product[6], lambda: leaves(par, 7), product[7]]
-        image = gather_and_multiply(par, tasks, work, panel[10:])
+        image = gather_and_multiply(par, tasks, work, panel[8:])
         buf[1 - par, pl.ds(0, BLOCK), :] = exact_dot(image, inverse[...], (((1,), (1,)), ((), ())))
         return carry
 

time: 131 us -> 131 us (level)
  no operation moved by 1% of the time
where the time goes in v16:
time: 131 us
  Pallas kernels  130 us (99%)
    pallas_call x1, Pallas kernels, per_device(): pl.pallas_call(kernel, out_shape=(narrow, narrow, broad), in_specs=[pl.Bl...  128 us

profile of v16, /device:TPU:1, one launch (start us, length us, event | category | flops | bytes accessed | tf_op | source)
XLA Modules:
  0.0 131.2 jit_solution(12794318847604799023)
XLA Ops:
  1.3 127.6 %iterate.1 = (f32[128,128]{1,0:T(8,128)}, f32[128,128]{1,0:T(8,128)}, f32[128,256]{1,0:T(8,128)}) custom-call(f32[128,16384]{1,0:T(8,128)} %kernel_hbm.1, f32[128,128]{1,0:T(8,128)} %start.1, f32[128,256]{1,0:T(8,128)} %test.1, s32[1]{0:T(128)S(6)} %copy.6.cutoff), custom_call_target="tpu_custom_call" | custom-call | flops 8589934592 | bytes 16777216 | tf_op jit(solution)/shard_map/iterate/pallas_call | solution.py:386
  128.9 2.3 %project.1 = (f32[128,128]{1,0:T(8,128)}, f32[128,256]{1,0:T(8,128)}) custom-call(f32[128,128]{1,0:T(8,128)} %get-tuple-element.5.image, f32[128,128]{1,0:T(8,128)} %get-tuple-element.6.inverse, f32[128,256]{1,0:T(8,128)} %get-tuple-element.7.kept), custom_call_target="tpu_custom_call" | custom-call | tf_op jit(solution)/shard_map/project/pallas_call | solution.py:431
